TPU v7x, 32 devices: a whole 2x2x4 slice. The times are simulated.
32 devices in a mesh: dp: 4 (over y, core), pipe: 4 (over z), tensor: 2 (over x).
Axes of the slice: x: 2, y: 2, z: 4, core: 2. Of those that a mesh axis runs over, the one named last changes fastest.
Arguments:
- inputs: bfloat16 [4, 1024, 8192], P('pipe', 'dp', 'tensor'), may hold values from -900 to 900
- norm_gain: float32 [4, 8192], P('pipe', 'tensor'), may hold values from 0.1 to 1.9
- value_weight: bfloat16 [4, 1024, 8192], P('pipe', None, 'tensor'), may hold values from -1 to 1
- value_cotangent: bfloat16 [4, 1024, 1024], P('pipe', 'dp'), may hold values from -6 to 6
- upper_grad: bfloat16 [4, 1024, 8192], P('pipe', 'dp', 'tensor'), may hold values from -3 to 3
Outputs:
- input_grad: bfloat16 [4, 1024, 8192], P('pipe', 'dp', 'tensor')
- weight_grad: float32 [4, 1024, 8192], P('pipe', 'dp', 'tensor')
- gain_grad: float32 [4, 8192], P('pipe', 'tensor')
All inputs are finite; a program needn't handle non-finite values.
Results may differ from a plain program's by a relative error of at most 0.014.
Values may be sent and summed in bfloat16 or wider, within the bound.
No kernel may reach another device: no remote copies, remote signals or barrier semaphores. Data moves between devices by JAX's collectives and lax.ppermute only.
A program may use at most 64 MiB of HBM per device.

v0:
```python
import jax
import jax.numpy as jnp
from jax import lax
from jax.sharding import PartitionSpec as P

D = 8192


def from_behind(array, axis, by):
    count = lax.axis_size(axis)
    pairs = [(i, i + by) for i in range(count) if 0 <= i + by < count]
    return lax.ppermute(array, axis, pairs)


def per_device(inputs, norm_gain, value_weight, value_cotangent, upper_grad):
    replicas = lax.axis_size("dp")
    grad_scale = float(inputs.shape[1] * replicas) ** (-0.5)
    received = from_behind(upper_grad, "pipe", -1)
    input_rows = inputs[0].astype(jnp.float32)
    gain_row = norm_gain[0]
    cotangent = value_cotangent[0]
    square_sum = lax.psum(jnp.sum(input_rows * input_rows, axis=1), "tensor")
    inverse_rms = lax.rsqrt(square_sum / D + 1e-05)[:, None]
    normed = input_rows * inverse_rms
    hidden = (normed * gain_row).astype(jnp.bfloat16)
    hidden_grad = jnp.dot(cotangent, value_weight[0], preferred_element_type=jnp.float32)
    center_sum = lax.psum(jnp.sum(gain_row * hidden_grad * normed, axis=1), "tensor")
    center = (center_sum / D)[:, None]
    weight_term = (
        lax.dot_general(
            cotangent, hidden, (((0,), (0,)), ((), ())), preferred_element_type=jnp.float32
        )
        * grad_scale
    )
    weight_grad = lax.psum_scatter(
        weight_term.astype(jnp.bfloat16), "dp", scatter_dimension=0, tiled=True
    ).astype(jnp.float32)
    local_grad = inverse_rms * (gain_row * hidden_grad - normed * center)
    input_grad = (local_grad + received[0].astype(jnp.float32)).astype(jnp.bfloat16)
    gain_grad = lax.psum(jnp.sum(hidden_grad * normed, axis=0) * grad_scale, "dp")
    return (input_grad[None], weight_grad[None], gain_grad[None])


def solution(mesh):
    return jax.shard_map(
        per_device,
        mesh=mesh,
        in_specs=(
            P("pipe", "dp", "tensor"),
            P("pipe", "tensor"),
            P("pipe", None, "tensor"),
            P("pipe", "dp", None),
            P("pipe", "dp", "tensor"),
        ),
        out_specs=(P("pipe", "dp", "tensor"), P("pipe", "dp", "tensor"), P("pipe", "tensor")),
        check_vma=False,
    )
```

profile of v0, /device:TPU:0, one launch (start us, length us, event | category | flops | bytes accessed | tf_op | source)
XLA Modules:
  0.0 112.6 jit_solution(17475725695721889067)
XLA Ops:
  7.2 0.0 copy-start
  7.2 0.0 reduce-scatter.2.cloned.1.call-start
  7.2 2.1 %fusion.14 = f32[256]{0:T(256)S(1)} fusion(bf16[1,256,4096]{2,1,0:T(8,128)(2,1)} %param.5), kind=kLoop, calls=%fused_computation.17 | loop fusion | flops 3145472 | bytes 2098176 | tf_op jit(solution)/shard_map/reduce_sum | solution.py:22
  9.4 5.8 %psum.21 = f32[256]{0:T(256)S(1)} all-reduce(f32[256]{0:T(256)S(1)} %fusion.14), channel_id=1, replica_groups=mesh['dp'=4,'pipe'=4,'tensor'=2] {'tensor'}, use_global_device_ids=true, to_apply=%region_1.0 | all-reduce | flops 256 | bytes 2048 | tf_op jit(solution)/shard_map/psum | solution.py:22
  15.2 0.0 copy-done
  15.2 7.4 %fusion.2 = bf16[1024,4096]{0,1:T(8,128)(2,1)} fusion(bf16[1,256,4096]{2,1,0:T(8,128)(2,1)} %param.5, f32[4096]{0:T(1024)} %bitcast.56, f32[256]{0:T(256)S(1)} %add_rsqrt_fusion, bf16[1,256,1024]{2,1,0:T(8,128)(2,1)S(1)} %copy-done), kind=kOutput, calls=%fused_computation.3 | convolution fusion | flops 2160066560 | bytes 11027456 | tf_op jit(solution)/shard_map/dot_general | solution.py:30
  22.6 0.0 copy-start.1
  22.6 0.0 copy-start.2
  22.6 0.0 reduce-scatter.2.cloned.1.call-update
  22.6 1.4 %collective-permute-start = (bf16[1,256,4096]{2,1,0:T(8,128)(2,1)}, bf16[1,256,4096]{2,1,0:T(8,128)(2,1)}, u32[]{:S(2)}, u32[]{:S(2)}) collective-permute-start(bf16[1,256,4096]{2,1,0:T(8,128)(2,1)} %param.9), channel_id=1, source_target_pairs={{2,0},{4,2},{6,4},{3,1},{5,3},{7,5},{10,8},{12,10},{14,12},{11,9},... | collective-permute-start | bytes 6291464 | tf_op jit(solution)/shard_map/ppermute | solution.py:12
  24.0 0.1 copy-done.1
  24.2 0.0 copy-done.2
  24.2 8.2 %fusion.13 = (f32[4096]{0:T(1024)S(1)}, f32[256]{0:T(256)S(1)}, f32[256,4096]{1,0:T(8,128)}) fusion(bf16[1,256,4096]{2,1,0:T(8,128)(2,1)S(1)} %copy-done.1, f32[256]{0:T(256)S(1)} %add_rsqrt_fusion, f32[4096]{0:T(1024)S(1)} %bitcast.57, bf16[1,1024,4096]{2,1,0:T(8,128)(2,1)} %param.7, bf16[1,256,1024]{2,1,0:T(8,128)(2,1)S(1)} %copy-done), kind=kOutput, calls=%fused_computation.16 | convolution fusion | flops 2154819328 | bytes 15239168 | tf_op jit(solution)/shard_map/dot_general | solution.py:26
  32.3 4.9 %psum.22 = f32[256]{0:T(256)S(1)} all-reduce(f32[256]{0:T(256)S(1)} %get-tuple-element.7), channel_id=1, replica_groups=mesh['dp'=4,'pipe'=4,'tensor'=2] {'tensor'}, use_global_device_ids=true, to_apply=%region_3.0 | all-reduce | flops 256 | bytes 2048 | tf_op jit(solution)/shard_map/psum | solution.py:27
  37.3 11.5 %psum.23 = f32[1,4096]{1,0:T(1,128)} all-reduce(f32[1,4096]{1,0:T(1,128)S(1)} %bitcast.55), channel_id=1, replica_groups=mesh['dp'=4,'pipe'=4,'tensor'=2] {'dp'}, use_global_device_ids=true, to_apply=%region_6.0 | all-reduce | flops 4096 | bytes 32768 | tf_op jit(solution)/shard_map/psum | solution.py:40
  48.8 22.8 %collective-permute-done = bf16[1,256,4096]{2,1,0:T(8,128)(2,1)} collective-permute-done((bf16[1,256,4096]{2,1,0:T(8,128)(2,1)}, bf16[1,256,4096]{2,1,0:T(8,128)(2,1)}, u32[]{:S(2)}, u32[]{:S(2)}) %collective-permute-start) | collective-permute-done | bytes 2097184 | tf_op jit(solution)/shard_map/ppermute | solution.py:12
  71.6 5.8 %fusion.19 = bf16[1,256,4096]{2,1,0:T(8,128)(2,1)} fusion(bf16[1,256,4096]{2,1,0:T(8,128)(2,1)S(1)} %copy-done.1, f32[256,4096]{1,0:T(8,128)} %get-tuple-element.8, bf16[1,256,4096]{2,1,0:T(8,128)(2,1)} %collective-permute-done, f32[256]{0:T(256)S(1)} %broadcast_multiply_fusion.1, f32[4096]{0:T(1024)S(1)} %bitcast.58, f32[256]{0:T(256)S(1)} %add_rsqrt_fusion), kind=kLoop, calls=%fused_computation.21 | loop fusion | flops 9437184 | bytes 10504192 | tf_op jit(solution)/shard_map/broadcast_in_dim | solution.py:41
  77.4 18.9 %reduce-scatter.2.cloned.1.call-done = bf16[256,4096]{0,1:T(8,128)(2,1)} async-done(((bf16[1024,4096]{0,1:T(8,128)(2,1)}), bf16[256,4096]{0,1:T(8,128)(2,1)}) %reduce-scatter.2.cloned.1.call-update) | async-done | bytes 2097168 | tf_op jit(solution)/shard_map/reduce_scatter | solution.py:35
  96.3 3.8 %bitcast_convert_fusion = f32[1,256,4096]{1,2,0:T(8,128)} fusion(bf16[256,4096]{0,1:T(8,128)(2,1)} %reduce-scatter.2.cloned.1.call-done), kind=kLoop, calls=%fused_computation.22 | loop fusion | flops 1048576 | bytes 6291456 | tf_op jit(solution)/shard_map/broadcast_in_dim | solution.py:41
  100.2 5.6 %copy.8 = f32[1,256,4096]{2,1,0:T(8,128)} copy(f32[1,256,4096]{1,2,0:T(8,128)} %bitcast_convert_fusion) | data formatting | bytes 8388608
  (3 shorter events, 0.0 us)
Async XLA Ops:
  7.2 8.0 %copy-start = (bf16[1,256,1024]{2,1,0:T(8,128)(2,1)S(1)}, bf16[1,256,1024]{2,1,0:T(8,128)(2,1)}, u32[]{:S(2)}) copy-start(bf16[1,256,1024]{2,1,0:T(8,128)(2,1)} %param.8) | copy-start | bytes 1572868
  7.2 89.1 %reduce-scatter.2.cloned.1.call-start = ((), (), s32[]{:S(2)}) async-start(), calls=%async_computation.1 | async-start | bytes 10485760 | tf_op jit(solution)/shard_map/reduce_scatter | solution.py:35
  22.6 1.6 %copy-start.1 = (bf16[1,256,4096]{2,1,0:T(8,128)(2,1)S(1)}, bf16[1,256,4096]{2,1,0:T(8,128)(2,1)}, u32[]{:S(2)}) copy-start(bf16[1,256,4096]{2,1,0:T(8,128)(2,1)} %param.5) | copy-start | bytes 6291460
  22.6 1.6 %copy-start.2 = (f32[1,4096]{1,0:T(1,128)S(1)}, f32[1,4096]{1,0:T(1,128)}, u32[]{:S(2)}) copy-start(f32[1,4096]{1,0:T(1,128)} %param.6) | copy-start | bytes 49156
  22.6 49.0 %collective-permute-start = (bf16[1,256,4096]{2,1,0:T(8,128)(2,1)}, bf16[1,256,4096]{2,1,0:T(8,128)(2,1)}, u32[]{:S(2)}, u32[]{:S(2)}) collective-permute-start(bf16[1,256,4096]{2,1,0:T(8,128)(2,1)} %param.9), channel_id=1, source_target_pairs={{2,0},{4,2},{6,4},{3,1},{5,3},{7,5},{10,8},{12,10},{14,12},{11,9},... | collective-permute-start | bytes 6291464 | tf_op jit(solution)/shard_map/ppermute | solution.py:12
Sparse Core Ops, SparseCore 0:
  22.7 73.5 reduce-scatter.1
where the time goes:
time: 113 us
  waiting for transfers between devices  41.7 us (37%)
  blocking collectives  22.3 us (20%)
  matrix products  15.5 us (14%)
  between operations  14.1 us (12%)
  other arithmetic  11.8 us (10%)
  local copies, waits for them, and re-layouts  5.74 us (5%)
  starting transfers between devices  1.46 us (1%)
    ppermute x1, waiting for transfers between devices, from_behind(): return lax.ppermute(array, axis, pairs)  22.8 us
    reduce_scatter x1, waiting for transfers between devices, per_device(): lax.psum_scatter(weight_term.astype(jnp.bfloat16), 'dp', scatter_dimensio...  18.9 us
    psum x1, blocking collectives, per_device(): lax.psum(jnp.sum(hidden_grad * normed, axis=0) * grad_scale, 'dp')  11.5 us
    broadcast_in_dim x2, other arithmetic, per_device(): return (input_grad[None], weight_grad[None], gain_grad[None])  9.68 us
    dot_general x1, matrix products, per_device(): jnp.dot(cotangent, value_weight[0], preferred_element_type=jnp.float32)  8.17 us
    dot_general x1, matrix products, per_device(): lax.dot_general(cotangent, hidden, (((0,), (0,)), ((), ())), preferred_el...  7.37 us
    psum x1, blocking collectives, per_device(): square_sum = lax.psum(jnp.sum(input_rows * input_rows, axis=1), 'tensor')  5.84 us
    unnamed x7, local copies, waits for them, and re-layouts  5.74 us
  transfers between devices with their start and end apart: 2, of which 2 were waited for; matrix products, arithmetic and copies ran while one was open for 12% of the time, Pallas kernels for 0%

commit v1 on v0

v1 whole, which is shorter than its diff:
```python
import functools

import jax
import jax.numpy as jnp
from jax import lax
from jax.experimental import pallas as pl
from jax.experimental.pallas import tpu as pltpu
from jax.sharding import PartitionSpec as P

D = 8192
EPS = 1e-05
Y_CHUNKS = 4
Z_CHUNKS = 4
MIB = 1 << 20


def after(value, *others):
    return lax.optimization_barrier((value,) + others)[0]


def shifted(array, axis, by):
    count = lax.axis_size(axis)
    return lax.ppermute(array, axis, [(i, (i + by) % count) for i in range(count)])


def sum_over(array, axis):
    total = array
    for by in range(1, lax.axis_size(axis)):
        total = total + shifted(array, axis, by)
    return total


class Replicas:
    def __init__(self, axis):
        self.axis = axis
        self.count = lax.axis_size(axis)
        self.width = 2 if self.count % 2 == 0 else 1
        self.groups = self.count // self.width

    def to(self, index, high, low):
        return (index // self.width + high) % self.groups * self.width + (index % self.width + low) % self.width

    def send(self, array, high, low):
        return lax.ppermute(array, self.axis, [(i, self.to(i, high, low)) for i in range(self.count)])


def square_sum_kernel(x_ref, out_ref):
    x = x_ref[...].astype(jnp.float32)
    out_ref[...] = jnp.sum(x * x, axis=1, keepdims=True)


def weight_kernel(sources, *refs):
    cots, blocks = refs[:sources], refs[sources : 2 * sources]
    gain_ref, out_ref = refs[2 * sources], refs[-1]
    total = None
    for cot, block in zip(cots, blocks):
        term = lax.dot_general(
            cot[...], block[...], (((0,), (0,)), ((), ())), preferred_element_type=jnp.float32
        )
        total = term if total is None else total + term
    out_ref[...] = total * gain_ref[...]


def weight_chunk(cots, own, received, gain_row, out, chunk, chunks):
    tokens, features = own.shape
    rows = cots[0].shape[1]
    width = features // chunks
    tile = min(width, 512)
    steps = width // tile
    first = chunk * steps
    sources = len(cots)
    whole = lambda c: (0, 0)
    placed = lambda c: (0, first + c)
    here = lambda c: (0, c)
    in_specs = [pl.BlockSpec((tokens, rows), whole)] * sources
    in_specs += [pl.BlockSpec((tokens, tile), placed)]
    in_specs += [pl.BlockSpec((tokens, tile), here)] * (sources - 1)
    in_specs += [pl.BlockSpec((1, tile), placed)]
    args = [*cots, own, *received, gain_row]
    aliases = {}
    if out is not None:
        in_specs.append(pl.BlockSpec(memory_space=pl.ANY))
        aliases = {len(args): 0}
        args.append(out)
    return pl.pallas_call(
        functools.partial(weight_kernel, sources),
        grid=(steps,),
        in_specs=in_specs,
        out_specs=pl.BlockSpec((rows, tile), placed),
        out_shape=jax.ShapeDtypeStruct((rows, features), jnp.float32),
        input_output_aliases=aliases,
        compiler_params=pltpu.CompilerParams(vmem_limit_bytes=32 * MIB),
        cost_estimate=pl.CostEstimate(
            flops=2 * sources * tokens * rows * width,
            bytes_accessed=2 * sources * tokens * (rows + width) + 4 * rows * width,
            transcendentals=0,
        ),
    )(*args)


def per_device(inputs, norm_gain, value_weight, value_cotangent, upper_grad):
    replicas = Replicas("dp")
    sections = lax.axis_size("pipe")
    x = inputs[0]
    tokens, features = x.shape
    gain_row = norm_gain
    cotangent = value_cotangent[0]
    rows = cotangent.shape[1] // replicas.count
    grad_scale = float(tokens * replicas.count) ** (-0.5)
    me = lax.axis_index("dp")

    down = [(i, i - 1) for i in range(1, sections)]
    height = tokens // Z_CHUNKS
    width = features // Y_CHUNKS

    far = [(high, 0) for high in range(1, replicas.groups)]
    near = [(0, low) for low in range(1, replicas.width)]

    upper = []
    gate = None
    for c in range(Z_CHUNKS):
        part = upper_grad[0, c * height : (c + 1) * height]
        if c >= 2:
            part = after(part, upper[c - 2])
        upper.append(lax.ppermute(part, "pipe", down))

    gathered = []
    for c in range(Y_CHUNKS):
        part = x[:, c * width : (c + 1) * width]
        if c >= 2:
            part = after(part, *gathered[c - 2][: len(far)])
        gathered.append([replicas.send(part, high, low) for high, low in far])
    near_x = [replicas.send(x, high, low) for high, low in near]
    sources = [(0, 0)] + near + far + [(high, low) for high, _ in far for _, low in near]

    square_sum = sum_over(jnp.sum(jnp.square(x.astype(jnp.float32)), axis=1), "tensor")
    inverse_rms = lax.rsqrt(square_sum / D + EPS)[:, None]

    scaled = (cotangent.astype(jnp.float32) * (inverse_rms * grad_scale)).astype(jnp.bfloat16)
    cots = []
    for high, low in sources:
        part = lax.dynamic_slice_in_dim(scaled, replicas.to(me, high, low) * rows, rows, axis=1)
        cots.append(part if (high, low) == (0, 0) else replicas.send(part, high, low))

    normed = x.astype(jnp.float32) * inverse_rms
    hidden_grad = jnp.dot(cotangent, value_weight[0], preferred_element_type=jnp.float32)
    product = hidden_grad * normed
    center = (sum_over(jnp.sum(gain_row * product, axis=1), "tensor") / D)[:, None]
    gain_local = jnp.sum(product, axis=0, keepdims=True) * grad_scale
    for high_low in (near, far):
        total = gain_local
        for high, low in high_low:
            total = total + replicas.send(gain_local, high, low)
        gain_local = total
    gain_grad = gain_local
    local_grad = inverse_rms * (gain_row * hidden_grad - normed * center)
    received = jnp.concatenate(upper, axis=0).astype(jnp.float32)
    input_grad = (local_grad + received).astype(jnp.bfloat16)

    weight_grad = None
    for c in range(Y_CHUNKS):
        passed = [replicas.send(block, 0, low) for block in gathered[c] for _, low in near]
        near_part = [block[:, c * width : (c + 1) * width] for block in near_x]
        weight_grad = weight_chunk(
            cots, x, near_part + gathered[c] + passed, gain_row, weight_grad, c, Y_CHUNKS
        )
    return (input_grad[None], weight_grad[None], gain_grad)


def solution(mesh):
    return jax.shard_map(
        per_device,
        mesh=mesh,
        in_specs=(
            P("pipe", "dp", "tensor"),
            P("pipe", "tensor"),
            P("pipe", None, "tensor"),
            P("pipe", "dp", None),
            P("pipe", "dp", "tensor"),
        ),
        out_specs=(P("pipe", "dp", "tensor"), P("pipe", "dp", "tensor"), P("pipe", "tensor")),
        check_vma=False,
    )
```

time: 113 us -> 85 us (0.75)
  blocking collectives: 22.3 us -> 0 us
  starting transfers between devices: 1.46 us -> 17.2 us
  between operations: 14.1 us -> 0.88 us
  Pallas kernels: 0 us -> 7.64 us
  matrix products: 15.5 us -> 8 us
  waiting for transfers between devices: 41.7 us -> 38.1 us
  other arithmetic: 11.8 us -> 8.21 us
    psum x3 -> x0, blocking collectives: 22.3 us -> none  [the longest x1 11.5 us: per_device(): lax.psum(jnp.sum(hidden_grad * normed, axis=0) * grad_scale, 'dp')]
    reduce_scatter x1 -> x0, waiting for transfers between devices: 18.9 us -> none  [per_device(): lax.psum_scatter(weight_term.astype(jnp.bfloat16), 'dp', scatter_dimensio...]
    ppermute x1 -> x20, starting transfers between devices: 1.42 us -> 17.2 us  [the longest x14 8.71 us: send(): lax.ppermute(array, self.axis, [(i, self.to(i, high, low)) for i in range...]
    ppermute x1 -> x20, waiting for transfers between devices: 22.8 us -> 38.1 us  [the longest x14 29.4 us: send(): lax.ppermute(array, self.axis, [(i, self.to(i, high, low)) for i in range...]
    pallas_call x0 -> x4, Pallas kernels: none -> 7.64 us  [weight_chunk(): pl.pallas_call(functools.partial(weight_kernel, sources), grid=(steps,),...]
    dot_general x1 -> x0, matrix products: 7.37 us -> none  [per_device(): lax.dot_general(cotangent, hidden, (((0,), (0,)), ((), ())), preferred_el...]
    unnamed x7 -> x8, local copies, waits for them, and re-layouts: 5.74 us -> 0.02 us
    broadcast_in_dim x2 -> x1, other arithmetic: 9.68 us -> 4.12 us  [per_device(): return (input_grad[None], weight_grad[None], gain_grad)]
  transfers between devices with their start and end apart: 2 -> 20, of which waited for: 2 -> 8; matrix products, arithmetic and copies ran while one was open for 12% -> 22% of each run, Pallas kernels for 0% -> 7%
where the time goes in v1:
time: 85 us; the launch traced here: 84.8 us
  waiting for transfers between devices  38.1 us (45%)
  starting transfers between devices  17.2 us (20%)
  other arithmetic  8.21 us (10%)
  matrix products  8 us (9%)
  Pallas kernels  7.64 us (9%)
  local copies, waits for them, and re-layouts  4.69 us (6%)
  between operations  0.88 us (1%)
    ppermute x14, waiting for transfers between devices, send(): lax.ppermute(array, self.axis, [(i, self.to(i, high, low)) for i in range...  29.4 us
    ppermute x14, starting transfers between devices, send(): lax.ppermute(array, self.axis, [(i, self.to(i, high, low)) for i in range...  8.71 us
    dot_general x1, matrix products, per_device(): jnp.dot(cotangent, value_weight[0], preferred_element_type=jnp.float32)  8 us
    pallas_call x4, Pallas kernels, weight_chunk(): pl.pallas_call(functools.partial(weight_kernel, sources), grid=(steps,),...  7.64 us
    ppermute x4, waiting for transfers between devices, per_device(): upper.append(lax.ppermute(part, 'pipe', down))  5.55 us
    ppermute x4, starting transfers between devices, per_device(): upper.append(lax.ppermute(part, 'pipe', down))  5.15 us
    broadcast_in_dim x1, other arithmetic, per_device(): return (input_grad[None], weight_grad[None], gain_grad)  4.12 us
    ppermute x2, starting transfers between devices, shifted(): lax.ppermute(array, axis, [(i, (i + by) % count) for i in range(count)])  3.38 us
  transfers between devices with their start and end apart: 20, of which 8 were waited for; matrix products, arithmetic and copies ran while one was open for 22% of the time, Pallas kernels for 7%

profile of v1, /device:TPU:0, one launch (start us, length us, event | category | flops | bytes accessed | tf_op | source)
XLA Modules:
  0.0 84.8 jit_solution(6753643276135949096)
XLA Ops:
  0.6 0.0 copy-start.2
  0.6 2.2 %fusion.8 = f32[256]{0:T(256)S(1)} fusion(bf16[1,256,4096]{2,1,0:T(8,128)(2,1)} %param.5), kind=kLoop, calls=%fused_computation.10 | loop fusion | flops 3145472 | bytes 2098176 | tf_op jit(solution)/shard_map/reduce_sum | solution.py:136
  2.9 3.0 %collective-permute-start = (f32[256]{0:T(256)S(1)}, f32[256]{0:T(256)S(1)}, u32[]{:S(2)}, u32[]{:S(2)}) collective-permute-start(f32[256]{0:T(256)S(1)} %fusion.8), channel_id=1, source_target_pairs={{0,1},{1,0},{2,3},{3,2},{4,5},{5,4},{6,7},{7,6},{8,9},{9,8},{10,11... | collective-permute-start | bytes 3080 | tf_op jit(solution)/shard_map/ppermute | solution.py:23
  5.9 0.0 copy-start
  5.9 0.0 copy-start.1
  5.9 0.0 copy-start.3
  5.9 3.0 %fusion.13 = (bf16[256,1024]{1,0:T(8,128)(2,1)}, bf16[256,1024]{1,0:T(8,128)(2,1)}, bf16[256,1024]{1,0:T(8,128)(2,1)}, bf16[256,1024]{1,0:T(8,128)(2,1)}) fusion(bf16[256,4096]{1,0:T(8,128)(2,1)} %bitcast.29), kind=kLoop, calls=%fused_computation.29 | loop fusion | bytes 4194304 | tf_op jit(solution)/shard_map/slice | solution.py:129
  8.9 1.5 %collective-permute-start.13 = (bf16[256,1024]{1,0:T(8,128)(2,1)}, bf16[256,1024]{1,0:T(8,128)(2,1)S(1)}, u32[]{:S(2)}, u32[]{:S(2)}) collective-permute-start(bf16[256,1024]{1,0:T(8,128)(2,1)} %get-tuple-element.19), channel_id=1, source_target_pairs={{0,16},{8,24},{16,0},{24,8},{1,17},{9,25},{17,1},{25,9},{2,18},{10... | collective-permute-start | bytes 1572872 | tf_op jit(solution)/shard_map/ppermute | solution.py:44
  10.4 0.5 collective-permute-start.10
  10.9 0.0 copy-done.2
  10.9 1.4 %slice_bitcast_fusion.3 = (bf16[64,4096]{1,0:T(8,128)(2,1)}, bf16[64,4096]{1,0:T(8,128)(2,1)}, bf16[64,4096]{1,0:T(8,128)(2,1)}, bf16[64,4096]{1,0:T(8,128)(2,1)}) fusion(bf16[1,256,4096]{2,1,0:T(8,128)(2,1)S(1)} %copy-done.2), kind=kLoop, calls=%fused_computation.19 | loop fusion | bytes 4194304 | tf_op jit(solution)/shard_map/squeeze | solution.py:122
  12.3 1.3 %collective-permute-start.2 = (bf16[64,4096]{1,0:T(8,128)(2,1)}, bf16[64,4096]{1,0:T(8,128)(2,1)}, u32[]{:S(2)}, u32[]{:S(2)}) collective-permute-start(bf16[64,4096]{1,0:T(8,128)(2,1)} %get-tuple-element.23), channel_id=1, source_target_pairs={{2,0},{4,2},{6,4},{3,1},{5,3},{7,5},{10,8},{12,10},{14,12},{11,9},... | collective-permute-start | bytes 1572872 | tf_op jit(solution)/shard_map/ppermute | solution.py:125
  13.6 1.3 %collective-permute-start.3 = (bf16[64,4096]{1,0:T(8,128)(2,1)}, bf16[64,4096]{1,0:T(8,128)(2,1)}, u32[]{:S(2)}, u32[]{:S(2)}) collective-permute-start(bf16[64,4096]{1,0:T(8,128)(2,1)} %get-tuple-element.24), channel_id=1, source_target_pairs={{2,0},{4,2},{6,4},{3,1},{5,3},{7,5},{10,8},{12,10},{14,12},{11,9},... | collective-permute-start | bytes 1572872 | tf_op jit(solution)/shard_map/ppermute | solution.py:125
  14.9 0.0 collective-permute-done
  14.9 0.0 copy-done
  14.9 0.0 copy-done.1
  14.9 0.0 copy-done.3
  14.9 8.0 %fusion.9 = (f32[4096]{0:T(1024)S(1)}, f32[256]{0:T(256)S(1)}, f32[256,4096]{1,0:T(8,128)}) fusion(f32[256]{0:T(256)S(1)} %get-tuple-element.14, bf16[1,256,4096]{2,1,0:T(8,128)(2,1)S(1)} %copy-done, f32[4096]{0:T(1024)S(1)} %bitcast.35, bf16[1,1024,4096]{2,1,0:T(8,128)(2,1)} %param.7, bf16[1,256,1024]{2,1,0:T(8,128)(2,1)S(1)} %copy-done.3), kind=kOutput, calls=%fused_computation.12 | convolution fusion | flops 2153770752 | bytes 15239168 | tf_op jit(solution)/shard_map/dot_general | solution.py:146
  22.9 0.0 collective-permute-start.18
  23.0 1.1 %collective-permute-done.18 = f32[1,4096]{1,0:T(1,128)S(1)} collective-permute-done((f32[1,4096]{1,0:T(1,128)S(1)}, f32[1,4096]{1,0:T(1,128)S(1)}, u32[]{:S(2)}, u32[]{:S(2)}) %collective-permute-start.18) | collective-permute-done | bytes 16416 | tf_op jit(solution)/shard_map/ppermute | solution.py:44
  24.1 0.2 collective-permute-start.9
  24.3 1.2 %multiply_convert_fusion = bf16[256,1024]{1,0:T(8,128)(2,1)S(1)} fusion(bf16[1,256,1024]{2,1,0:T(8,128)(2,1)} %param.8, f32[256]{0:T(256)S(1)} %get-tuple-element.13), kind=kLoop, calls=%fused_computation.14 | loop fusion | flops 786432 | bytes 1049600 | tf_op jit(solution)/shard_map/convert_element_type | solution.py:139
  25.5 0.1 constant_dynamic-slice_fusion
  25.6 0.0 collective-permute-done.13.refs_6_
  25.6 0.4 collective-permute-start.6
  26.0 7.7 %collective-permute-done.10.refs_6_ = bf16[256,1024]{1,0:T(8,128)(2,1)S(1)} collective-permute-done((bf16[256,1024]{1,0:T(8,128)(2,1)}, bf16[256,1024]{1,0:T(8,128)(2,1)S(1)}, u32[]{:S(2)}, u32[]{:S(2)}) %collective-permute-start.10) | collective-permute-done | bytes 524320 | tf_op jit(solution)/shard_map/ppermute | solution.py:44
  33.7 1.5 %collective-permute-start.7 = (bf16[256,256]{1,0:T(8,128)(2,1)S(1)}, bf16[256,256]{1,0:T(8,128)(2,1)S(1)}, u32[]{:S(2)}, u32[]{:S(2)}) collective-permute-start(bf16[256,256]{1,0:T(8,128)(2,1)S(1)} %get-tuple-element.28), channel_id=1, source_target_pairs={{0,16},{8,24},{16,0},{24,8},{1,17},{9,25},{17,1},{25,9},{2,18},{10... | collective-permute-start | bytes 393224 | tf_op jit(solution)/shard_map/ppermute | solution.py:44
  35.3 0.0 collective-permute-done.2
  35.3 0.6 collective-permute-start.19
  35.8 2.7 %collective-permute-done.3 = bf16[64,4096]{1,0:T(8,128)(2,1)} collective-permute-done((bf16[64,4096]{1,0:T(8,128)(2,1)}, bf16[64,4096]{1,0:T(8,128)(2,1)}, u32[]{:S(2)}, u32[]{:S(2)}) %collective-permute-start.3) | collective-permute-done | bytes 524320 | tf_op jit(solution)/shard_map/ppermute | solution.py:125
  38.5 0.4 collective-permute-start.1
  38.9 3.2 %collective-permute-done.1 = f32[256]{0:T(256)S(1)} collective-permute-done((f32[256]{0:T(256)S(1)}, f32[256]{0:T(256)S(1)}, u32[]{:S(2)}, u32[]{:S(2)}) %collective-permute-start.1) | collective-permute-done | bytes 1056 | tf_op jit(solution)/shard_map/ppermute | solution.py:23
  42.1 1.5 %collective-permute-start.14 = (bf16[256,1024]{1,0:T(8,128)(2,1)}, bf16[256,1024]{1,0:T(8,128)(2,1)S(1)}, u32[]{:S(2)}, u32[]{:S(2)}) collective-permute-start(bf16[256,1024]{1,0:T(8,128)(2,1)} %get-tuple-element.10), channel_id=1, source_target_pairs={{0,16},{8,24},{16,0},{24,8},{1,17},{9,25},{17,1},{25,9},{2,18},{10... | collective-permute-start | bytes 1572872 | tf_op jit(solution)/shard_map/ppermute | solution.py:44
  43.6 0.0 collective-permute-done.19
  43.6 0.5 collective-permute-start.11
  44.1 0.0 collective-permute-done.6.refs_1_
  44.1 1.3 %collective-permute-start.4 = (bf16[64,4096]{1,0:T(8,128)(2,1)}, bf16[64,4096]{1,0:T(8,128)(2,1)S(1)}, u32[]{:S(2)}, u32[]{:S(2)}) collective-permute-start(bf16[64,4096]{1,0:T(8,128)(2,1)} %get-tuple-element.7), channel_id=1, source_target_pairs={{2,0},{4,2},{6,4},{3,1},{5,3},{7,5},{10,8},{12,10},{14,12},{11,9},... | collective-permute-start | bytes 1572872 | tf_op jit(solution)/shard_map/ppermute | solution.py:125
  45.4 0.0 collective-permute-done.7.refs_2_
  45.4 1.3 %collective-permute-start.5 = (bf16[64,4096]{1,0:T(8,128)(2,1)}, bf16[64,4096]{1,0:T(8,128)(2,1)S(1)}, u32[]{:S(2)}, u32[]{:S(2)}) collective-permute-start(bf16[64,4096]{1,0:T(8,128)(2,1)} %get-tuple-element.8), channel_id=1, source_target_pairs={{2,0},{4,2},{6,4},{3,1},{5,3},{7,5},{10,8},{12,10},{14,12},{11,9},... | collective-permute-start | bytes 1572872 | tf_op jit(solution)/shard_map/ppermute | solution.py:125
  46.8 0.6 add.98
  47.4 9.8 %collective-permute-done.14.refs_6_ = bf16[256,1024]{1,0:T(8,128)(2,1)S(1)} collective-permute-done((bf16[256,1024]{1,0:T(8,128)(2,1)}, bf16[256,1024]{1,0:T(8,128)(2,1)S(1)}, u32[]{:S(2)}, u32[]{:S(2)}) %collective-permute-start.14) | collective-permute-done | bytes 524320 | tf_op jit(solution)/shard_map/ppermute | solution.py:44
  57.2 0.0 collective-permute-start.17
  57.2 7.3 %collective-permute-done.11.refs_6_ = bf16[256,1024]{1,0:T(8,128)(2,1)S(1)} collective-permute-done((bf16[256,1024]{1,0:T(8,128)(2,1)}, bf16[256,1024]{1,0:T(8,128)(2,1)S(1)}, u32[]{:S(2)}, u32[]{:S(2)}) %collective-permute-start.11) | collective-permute-done | bytes 524320 | tf_op jit(solution)/shard_map/ppermute | solution.py:44
  64.5 0.0 collective-permute-start.16
  64.5 0.0 collective-permute-done.4
  64.5 0.5 collective-permute-start.15
  65.0 2.8 %collective-permute-done.5 = bf16[64,4096]{1,0:T(8,128)(2,1)S(1)} collective-permute-done((bf16[64,4096]{1,0:T(8,128)(2,1)}, bf16[64,4096]{1,0:T(8,128)(2,1)S(1)}, u32[]{:S(2)}, u32[]{:S(2)}) %collective-permute-start.5) | collective-permute-done | bytes 524320 | tf_op jit(solution)/shard_map/ppermute | solution.py:125
  67.8 0.0 collective-permute-start.12
  67.8 4.1 %fusion.10 = bf16[1,256,4096]{2,1,0:T(8,128)(2,1)} fusion(f32[256,4096]{1,0:T(8,128)} %get-tuple-element.31, bf16[64,4096]{1,0:T(8,128)(2,1)S(1)} %collective-permute-done.5, bf16[64,4096]{1,0:T(8,128)(2,1)S(1)} %collective-permute-done.4, bf16[64,4096]{1,0:T(8,128)(2,1)} %collective-permute-done.3, bf16[64,4096]{1,0:T(8,128)(2,1)} %collective-permute-done.2, ...), kind=kLoop, calls=%fused_computation.13 | loop fusion | flops 16777216 | bytes 10504192 | tf_op jit(solution)/shard_map/broadcast_in_dim | solution.py:167
  71.9 0.0 collective-permute-done.9
  71.9 1.5 %collective-permute-start.8 = (bf16[256,256]{1,0:T(8,128)(2,1)S(1)}, bf16[256,256]{1,0:T(8,128)(2,1)S(1)}, u32[]{:S(2)}, u32[]{:S(2)}) collective-permute-start(bf16[256,256]{1,0:T(8,128)(2,1)S(1)} %get-tuple-element.27), channel_id=1, source_target_pairs={{0,24},{8,16},{16,8},{24,0},{1,25},{9,17},{17,9},{25,1},{2,26},{10... | collective-permute-start | bytes 393224 | tf_op jit(solution)/shard_map/ppermute | solution.py:44
  73.4 0.2 fusion.12
  73.6 3.4 %collective-permute-done.8.refs_3_ = bf16[256,256]{1,0:T(8,128)(2,1)S(1)} collective-permute-done((bf16[256,256]{1,0:T(8,128)(2,1)S(1)}, bf16[256,256]{1,0:T(8,128)(2,1)S(1)}, u32[]{:S(2)}, u32[]{:S(2)}) %collective-permute-start.8) | collective-permute-done | bytes 131104 | tf_op jit(solution)/shard_map/ppermute | solution.py:44
  77.1 0.0 collective-permute-done.17.refs_7_
  77.1 1.9 %shard_map.76.refs_9_ = f32[256,4096]{1,0:T(8,128)} custom-call(bf16[256,256]{1,0:T(8,128)(2,1)S(1)} %get-tuple-element.30.refs_0_, bf16[256,256]{1,0:T(8,128)(2,1)S(1)} %collective-permute-done.6.refs_1_, bf16[256,256]{1,0:T(8,128)(2,1)S(1)} %collective-permute-done.7.refs_2_, bf16[256,256]{1,0:T(8,128)(2,1)S(1)} %collective-permute-done.8.refs_3_, ...), custom_call_target="tpu_custom_call" | custom-call | flops 536870912 | bytes 3670016 | tf_op jit(solution)/shard_map/pallas_call | solution.py:85
  79.0 0.0 collective-permute-done.16.refs_7_
  79.0 1.9 %shard_map.77.refs_9_ = f32[256,4096]{1,0:T(8,128)} custom-call(bf16[256,256]{1,0:T(8,128)(2,1)S(1)} %get-tuple-element.30.refs_0_, bf16[256,256]{1,0:T(8,128)(2,1)S(1)} %collective-permute-done.6.refs_1_, bf16[256,256]{1,0:T(8,128)(2,1)S(1)} %collective-permute-done.7.refs_2_, ...), custom_call_target="tpu_custom_call", output_to_operand_aliasing={{}: (9, {})} | custom-call | flops 536870912 | bytes 3670016 | tf_op jit(solution)/shard_map/pallas_call | solution.py:85
  80.9 0.0 collective-permute-done.15.refs_7_
  80.9 1.9 %shard_map.78.refs_9_ = f32[256,4096]{1,0:T(8,128)} custom-call(bf16[256,256]{1,0:T(8,128)(2,1)S(1)} %get-tuple-element.30.refs_0_, bf16[256,256]{1,0:T(8,128)(2,1)S(1)} %collective-permute-done.6.refs_1_, bf16[256,256]{1,0:T(8,128)(2,1)S(1)} %collective-permute-done.7.refs_2_, ...), custom_call_target="tpu_custom_call", output_to_operand_aliasing={{}: (9, {})} | custom-call | flops 536870912 | bytes 3670016 | tf_op jit(solution)/shard_map/pallas_call | solution.py:85
  82.8 0.0 collective-permute-done.12.refs_7_
  82.8 1.9 %shard_map.79 = f32[256,4096]{1,0:T(8,128)} custom-call(bf16[256,256]{1,0:T(8,128)(2,1)S(1)} %get-tuple-element.30.refs_0_, bf16[256,256]{1,0:T(8,128)(2,1)S(1)} %collective-permute-done.6.refs_1_, bf16[256,256]{1,0:T(8,128)(2,1)S(1)} %collective-permute-done.7.refs_2_, ...), custom_call_target="tpu_custom_call", output_to_operand_aliasing={{}: (9, {})} | custom-call | flops 536870912 | bytes 3670016 | tf_op jit(solution)/shard_map/pallas_call | solution.py:85
  (4 shorter events, 0.0 us)
Async XLA Ops:
  0.6 10.3 %copy-start.2 = (bf16[1,256,4096]{2,1,0:T(8,128)(2,1)S(1)}, bf16[1,256,4096]{2,1,0:T(8,128)(2,1)}, u32[]{:S(2)}) copy-start(bf16[1,256,4096]{2,1,0:T(8,128)(2,1)} %param.9) | copy-start | bytes 6291460
  2.9 12.0 %collective-permute-start = (f32[256]{0:T(256)S(1)}, f32[256]{0:T(256)S(1)}, u32[]{:S(2)}, u32[]{:S(2)}) collective-permute-start(f32[256]{0:T(256)S(1)} %fusion.8), channel_id=1, source_target_pairs={{0,1},{1,0},{2,3},{3,2},{4,5},{5,4},{6,7},{7,6},{8,9},{9,8},{10,11... | collective-permute-start | bytes 3080 | tf_op jit(solution)/shard_map/ppermute | solution.py:23
  5.9 9.0 %copy-start = (bf16[1,256,4096]{2,1,0:T(8,128)(2,1)S(1)}, bf16[1,256,4096]{2,1,0:T(8,128)(2,1)}, u32[]{:S(2)}) copy-start(bf16[1,256,4096]{2,1,0:T(8,128)(2,1)} %param.5) | copy-start | bytes 6291460
  5.9 9.0 %copy-start.1 = (f32[1,4096]{1,0:T(1,128)S(1)}, f32[1,4096]{1,0:T(1,128)}, u32[]{:S(2)}) copy-start(f32[1,4096]{1,0:T(1,128)} %refs_8_.7) | copy-start | bytes 49156
  5.9 9.0 %copy-start.3 = (bf16[1,256,1024]{2,1,0:T(8,128)(2,1)S(1)}, bf16[1,256,1024]{2,1,0:T(8,128)(2,1)}, u32[]{:S(2)}) copy-start(bf16[1,256,1024]{2,1,0:T(8,128)(2,1)} %param.8) | copy-start | bytes 1572868
  8.9 16.7 %collective-permute-start.13 = (bf16[256,1024]{1,0:T(8,128)(2,1)}, bf16[256,1024]{1,0:T(8,128)(2,1)S(1)}, u32[]{:S(2)}, u32[]{:S(2)}) collective-permute-start(bf16[256,1024]{1,0:T(8,128)(2,1)} %get-tuple-element.19), channel_id=1, source_target_pairs={{0,16},{8,24},{16,0},{24,8},{1,17},{9,25},{17,1},{25,9},{2,18},{10... | collective-permute-start | bytes 1572872 | tf_op jit(solution)/shard_map/ppermute | solution.py:44
  10.4 23.3 %collective-permute-start.10 = (bf16[256,1024]{1,0:T(8,128)(2,1)}, bf16[256,1024]{1,0:T(8,128)(2,1)S(1)}, u32[]{:S(2)}, u32[]{:S(2)}) collective-permute-start(bf16[256,1024]{1,0:T(8,128)(2,1)} %get-tuple-element.21), channel_id=1, source_target_pairs={{0,16},{8,24},{16,0},{24,8},{1,17},{9,25},{17,1},{25,9},{2,18},{10... | collective-permute-start | bytes 1572872 | tf_op jit(solution)/shard_map/ppermute | solution.py:44
  12.3 23.0 %collective-permute-start.2 = (bf16[64,4096]{1,0:T(8,128)(2,1)}, bf16[64,4096]{1,0:T(8,128)(2,1)}, u32[]{:S(2)}, u32[]{:S(2)}) collective-permute-start(bf16[64,4096]{1,0:T(8,128)(2,1)} %get-tuple-element.23), channel_id=1, source_target_pairs={{2,0},{4,2},{6,4},{3,1},{5,3},{7,5},{10,8},{12,10},{14,12},{11,9},... | collective-permute-start | bytes 1572872 | tf_op jit(solution)/shard_map/ppermute | solution.py:125
  13.6 25.0 %collective-permute-start.3 = (bf16[64,4096]{1,0:T(8,128)(2,1)}, bf16[64,4096]{1,0:T(8,128)(2,1)}, u32[]{:S(2)}, u32[]{:S(2)}) collective-permute-start(bf16[64,4096]{1,0:T(8,128)(2,1)} %get-tuple-element.24), channel_id=1, source_target_pairs={{2,0},{4,2},{6,4},{3,1},{5,3},{7,5},{10,8},{12,10},{14,12},{11,9},... | collective-permute-start | bytes 1572872 | tf_op jit(solution)/shard_map/ppermute | solution.py:125
  22.9 1.2 %collective-permute-start.18 = (f32[1,4096]{1,0:T(1,128)S(1)}, f32[1,4096]{1,0:T(1,128)S(1)}, u32[]{:S(2)}, u32[]{:S(2)}) collective-permute-start(f32[1,4096]{1,0:T(1,128)S(1)} %bitcast.38), channel_id=1, source_target_pairs={{0,8},{8,0},{16,24},{24,16},{1,9},{9,1},{17,25},{25,17},{2,10},{10... | collective-permute-start | bytes 49160 | tf_op jit(solution)/shard_map/ppermute | solution.py:44
  24.1 47.8 %collective-permute-start.9 = (bf16[256,4096]{1,0:T(8,128)(2,1)S(1)}, bf16[256,4096]{1,0:T(8,128)(2,1)S(1)}, u32[]{:S(2)}, u32[]{:S(2)}) collective-permute-start(bf16[256,4096]{1,0:T(8,128)(2,1)S(1)} %bitcast.30), channel_id=1, source_target_pairs={{0,8},{8,0},{16,24},{24,16},{1,9},{9,1},{17,25},{25,17},{2,10},{10... | collective-permute-start | bytes 6291464 | tf_op jit(solution)/shard_map/ppermute | solution.py:44
  25.6 18.6 %collective-permute-start.6 = (bf16[256,256]{1,0:T(8,128)(2,1)S(1)}, bf16[256,256]{1,0:T(8,128)(2,1)S(1)}, u32[]{:S(2)}, u32[]{:S(2)}) collective-permute-start(bf16[256,256]{1,0:T(8,128)(2,1)S(1)} %get-tuple-element.29), channel_id=1, source_target_pairs={{0,8},{8,0},{16,24},{24,16},{1,9},{9,1},{17,25},{25,17},{2,10},{10... | collective-permute-start | bytes 393224 | tf_op jit(solution)/shard_map/ppermute | solution.py:44
  33.7 11.7 %collective-permute-start.7 = (bf16[256,256]{1,0:T(8,128)(2,1)S(1)}, bf16[256,256]{1,0:T(8,128)(2,1)S(1)}, u32[]{:S(2)}, u32[]{:S(2)}) collective-permute-start(bf16[256,256]{1,0:T(8,128)(2,1)S(1)} %get-tuple-element.28), channel_id=1, source_target_pairs={{0,16},{8,24},{16,0},{24,8},{1,17},{9,25},{17,1},{25,9},{2,18},{10... | collective-permute-start | bytes 393224 | tf_op jit(solution)/shard_map/ppermute | solution.py:44
  35.3 8.4 %collective-permute-start.19 = (f32[1,4096]{1,0:T(1,128)S(1)}, f32[1,4096]{1,0:T(1,128)S(1)}, u32[]{:S(2)}, u32[]{:S(2)}) collective-permute-start(f32[1,4096]{1,0:T(1,128)S(1)} %add.97), channel_id=1, source_target_pairs={{0,16},{8,24},{16,0},{24,8},{1,17},{9,25},{17,1},{25,9},{2,18},{10... | collective-permute-start | bytes 49160 | tf_op jit(solution)/shard_map/ppermute | solution.py:44
  38.5 3.6 %collective-permute-start.1 = (f32[256]{0:T(256)S(1)}, f32[256]{0:T(256)S(1)}, u32[]{:S(2)}, u32[]{:S(2)}) collective-permute-start(f32[256]{0:T(256)S(1)} %get-tuple-element.12), channel_id=1, source_target_pairs={{0,1},{1,0},{2,3},{3,2},{4,5},{5,4},{6,7},{7,6},{8,9},{9,8},{10,11... | collective-permute-start | bytes 3080 | tf_op jit(solution)/shard_map/ppermute | solution.py:23
  42.1 15.1 %collective-permute-start.14 = (bf16[256,1024]{1,0:T(8,128)(2,1)}, bf16[256,1024]{1,0:T(8,128)(2,1)S(1)}, u32[]{:S(2)}, u32[]{:S(2)}) collective-permute-start(bf16[256,1024]{1,0:T(8,128)(2,1)} %get-tuple-element.10), channel_id=1, source_target_pairs={{0,16},{8,24},{16,0},{24,8},{1,17},{9,25},{17,1},{25,9},{2,18},{10... | collective-permute-start | bytes 1572872 | tf_op jit(solution)/shard_map/ppermute | solution.py:44
  43.6 20.8 %collective-permute-start.11 = (bf16[256,1024]{1,0:T(8,128)(2,1)}, bf16[256,1024]{1,0:T(8,128)(2,1)S(1)}, u32[]{:S(2)}, u32[]{:S(2)}) collective-permute-start(bf16[256,1024]{1,0:T(8,128)(2,1)} %get-tuple-element.9), channel_id=1, source_target_pairs={{0,16},{8,24},{16,0},{24,8},{1,17},{9,25},{17,1},{25,9},{2,18},{10... | collective-permute-start | bytes 1572872 | tf_op jit(solution)/shard_map/ppermute | solution.py:44
  44.1 20.3 %collective-permute-start.4 = (bf16[64,4096]{1,0:T(8,128)(2,1)}, bf16[64,4096]{1,0:T(8,128)(2,1)S(1)}, u32[]{:S(2)}, u32[]{:S(2)}) collective-permute-start(bf16[64,4096]{1,0:T(8,128)(2,1)} %get-tuple-element.7), channel_id=1, source_target_pairs={{2,0},{4,2},{6,4},{3,1},{5,3},{7,5},{10,8},{12,10},{14,12},{11,9},... | collective-permute-start | bytes 1572872 | tf_op jit(solution)/shard_map/ppermute | solution.py:125
  45.4 22.4 %collective-permute-start.5 = (bf16[64,4096]{1,0:T(8,128)(2,1)}, bf16[64,4096]{1,0:T(8,128)(2,1)S(1)}, u32[]{:S(2)}, u32[]{:S(2)}) collective-permute-start(bf16[64,4096]{1,0:T(8,128)(2,1)} %get-tuple-element.8), channel_id=1, source_target_pairs={{2,0},{4,2},{6,4},{3,1},{5,3},{7,5},{10,8},{12,10},{14,12},{11,9},... | collective-permute-start | bytes 1572872 | tf_op jit(solution)/shard_map/ppermute | solution.py:125
  57.2 19.9 %collective-permute-start.17 = (bf16[256,1024]{1,0:T(8,128)(2,1)S(1)}, bf16[256,1024]{1,0:T(8,128)(2,1)S(1)}, u32[]{:S(2)}, u32[]{:S(2)}) collective-permute-start(bf16[256,1024]{1,0:T(8,128)(2,1)S(1)} %collective-permute-done.13.refs_6_), channel_id=1, source_target_pairs={{0,8},{8,0},{16,24},{24,16},{1,9},{9,1},{17,25},{25,17},{2,10},{10... | collective-permute-start | bytes 1572872 | tf_op jit(solution)/shard_map/ppermute | solution.py:44
  64.5 14.5 %collective-permute-start.16 = (bf16[256,1024]{1,0:T(8,128)(2,1)S(1)}, bf16[256,1024]{1,0:T(8,128)(2,1)S(1)}, u32[]{:S(2)}, u32[]{:S(2)}) collective-permute-start(bf16[256,1024]{1,0:T(8,128)(2,1)S(1)} %collective-permute-done.10.refs_6_), channel_id=1, source_target_pairs={{0,8},{8,0},{16,24},{24,16},{1,9},{9,1},{17,25},{25,17},{2,10},{10... | collective-permute-start | bytes 1572872 | tf_op jit(solution)/shard_map/ppermute | solution.py:44
  64.5 16.5 %collective-permute-start.15 = (bf16[256,1024]{1,0:T(8,128)(2,1)S(1)}, bf16[256,1024]{1,0:T(8,128)(2,1)S(1)}, u32[]{:S(2)}, u32[]{:S(2)}) collective-permute-start(bf16[256,1024]{1,0:T(8,128)(2,1)S(1)} %collective-permute-done.14.refs_6_), channel_id=1, source_target_pairs={{0,8},{8,0},{16,24},{24,16},{1,9},{9,1},{17,25},{25,17},{2,10},{10... | collective-permute-start | bytes 1572872 | tf_op jit(solution)/shard_map/ppermute | solution.py:44
  67.8 15.0 %collective-permute-start.12 = (bf16[256,1024]{1,0:T(8,128)(2,1)S(1)}, bf16[256,1024]{1,0:T(8,128)(2,1)S(1)}, u32[]{:S(2)}, u32[]{:S(2)}) collective-permute-start(bf16[256,1024]{1,0:T(8,128)(2,1)S(1)} %collective-permute-done.11.refs_6_), channel_id=1, source_target_pairs={{0,8},{8,0},{16,24},{24,16},{1,9},{9,1},{17,25},{25,17},{2,10},{10... | collective-permute-start | bytes 1572872 | tf_op jit(solution)/shard_map/ppermute | solution.py:44
  71.9 5.2 %collective-permute-start.8 = (bf16[256,256]{1,0:T(8,128)(2,1)S(1)}, bf16[256,256]{1,0:T(8,128)(2,1)S(1)}, u32[]{:S(2)}, u32[]{:S(2)}) collective-permute-start(bf16[256,256]{1,0:T(8,128)(2,1)S(1)} %get-tuple-element.27), channel_id=1, source_target_pairs={{0,24},{8,16},{16,8},{24,0},{1,25},{9,17},{17,9},{25,1},{2,26},{10... | collective-permute-start | bytes 393224 | tf_op jit(solution)/shard_map/ppermute | solution.py:44

commit v2 on v1

v2 whole, which is shorter than its diff:
```python
import functools

import jax
import jax.numpy as jnp
from jax import lax
from jax.experimental import pallas as pl
from jax.experimental.pallas import tpu as pltpu
from jax.sharding import PartitionSpec as P

D = 8192
EPS = 1e-05
Y_PARTS = (5, 3)
MIB = 1 << 20
PARAMS = pltpu.CompilerParams(vmem_limit_bytes=24 * MIB)


def after(value, *others):
    return lax.optimization_barrier((value,) + others)[0]


def spans(total, parts):
    unit = total // sum(parts)
    ends = [unit * sum(parts[: i + 1]) for i in range(len(parts))]
    return list(zip([0] + ends[:-1], [unit * p for p in parts]))


def tile_of(width, largest):
    tile = min(width, largest)
    while width % tile:
        tile //= 2
    return tile


def from_others(array, axis):
    count = lax.axis_size(axis)
    return [lax.ppermute(array, axis, [(i, (i + by) % count) for i in range(count)]) for by in range(1, count)]


class Replicas:
    def __init__(self, axis):
        self.axis = axis
        self.count = lax.axis_size(axis)
        self.width = 2 if self.count % 2 == 0 else 1
        self.groups = self.count // self.width
        self.high = lax.axis_index(axis) // self.width
        self.low = lax.axis_index(axis) % self.width

    def to(self, index, high, low):
        return (index // self.width + high) % self.groups * self.width + (index % self.width + low) % self.width

    def send(self, array, high, low):
        return lax.ppermute(array, self.axis, [(i, self.to(i, high, low)) for i in range(self.count)])


def lanes_to_row(sums):
    return jnp.sum(sums.T, axis=0, keepdims=True)


def row_to_column(row):
    return jnp.broadcast_to(row, (128, row.shape[1])).T[:, :1]


def fold_lanes(array):
    total = array[:, :128]
    for at in range(128, array.shape[1], 128):
        total = total + array[:, at : at + 128]
    return total


def grad_kernel(cot_ref, weight_ref, x_ref, gain_ref, hidden_grad_ref, sums_ref, squares, centers):
    step = pl.program_id(0)

    @pl.when(step == 0)
    def _():
        squares[...] = jnp.zeros_like(squares)
        centers[...] = jnp.zeros_like(centers)

    x = x_ref[...].astype(jnp.float32)
    hidden_grad = jnp.dot(cot_ref[...], weight_ref[...], preferred_element_type=jnp.float32)
    hidden_grad_ref[...] = hidden_grad
    squares[...] += fold_lanes(x * x)
    centers[...] += fold_lanes(gain_ref[...] * hidden_grad * x)

    @pl.when(step == pl.num_programs(0) - 1)
    def _():
        sums_ref[0:1] = lanes_to_row(squares[...])
        sums_ref[1:2] = lanes_to_row(centers[...])


def hidden_grad_and_sums(cotangent, weight, x, gain_row):
    tokens, features = x.shape
    tile = tile_of(features, 512)
    column = lambda c: (0, c)
    whole = lambda c: (0, 0)
    return pl.pallas_call(
        grad_kernel,
        grid=(features // tile,),
        in_specs=[
            pl.BlockSpec(cotangent.shape, whole),
            pl.BlockSpec((weight.shape[0], tile), column),
            pl.BlockSpec((tokens, tile), column),
            pl.BlockSpec((1, tile), column),
        ],
        out_specs=[pl.BlockSpec((tokens, tile), column), pl.BlockSpec((2, tokens), whole)],
        out_shape=[
            jax.ShapeDtypeStruct((tokens, features), jnp.float32),
            jax.ShapeDtypeStruct((2, tokens), jnp.float32),
        ],
        scratch_shapes=[pltpu.VMEM((tokens, 128), jnp.float32)] * 2,
        compiler_params=PARAMS,
        cost_estimate=pl.CostEstimate(
            flops=2 * tokens * features * weight.shape[0],
            bytes_accessed=2 * (weight.size + cotangent.size + x.size) + 4 * x.size,
            transcendentals=0,
        ),
    )(cotangent, weight, x, gain_row)


def local_kernel(scale, others, *refs):
    sums_refs = refs[: others + 1]
    cot_ref, x_ref, hidden_grad_ref, gain_ref = refs[others + 1 : others + 5]
    local_ref, gain_grad_ref, scaled_ref, inverse, factor = refs[others + 5 :]

    @pl.when(pl.program_id(0) == 0)
    def _():
        sums = sums_refs[0][...]
        for ref in sums_refs[1:]:
            sums = sums + ref[...]
        inverse_row = lax.rsqrt(sums[0:1] / D + EPS)
        center_row = inverse_row * sums[1:2] / D
        inverse[...] = row_to_column(inverse_row)
        factor[...] = row_to_column(inverse_row * center_row)
        scaled_ref[...] = (cot_ref[...].astype(jnp.float32) * (inverse[...] * scale)).astype(jnp.bfloat16)

    x = x_ref[...].astype(jnp.float32)
    hidden_grad = hidden_grad_ref[...]
    local_ref[...] = inverse[...] * (gain_ref[...] * hidden_grad - x * factor[...])
    gain_grad_ref[...] = jnp.sum(hidden_grad * x * inverse[...], axis=0, keepdims=True) * scale


def local_terms(sums, cotangent, x, hidden_grad, gain_row, scale):
    tokens, features = x.shape
    tile = tile_of(features, 512)
    column = lambda c: (0, c)
    whole = lambda c: (0, 0)
    return pl.pallas_call(
        functools.partial(local_kernel, scale, len(sums) - 1),
        grid=(features // tile,),
        in_specs=[pl.BlockSpec((2, tokens), whole)] * len(sums)
        + [
            pl.BlockSpec(cotangent.shape, whole),
            pl.BlockSpec((tokens, tile), column),
            pl.BlockSpec((tokens, tile), column),
            pl.BlockSpec((1, tile), column),
        ],
        out_specs=[
            pl.BlockSpec((tokens, tile), column),
            pl.BlockSpec((1, tile), column),
            pl.BlockSpec(cotangent.shape, whole),
        ],
        out_shape=[
            jax.ShapeDtypeStruct((tokens, features), jnp.float32),
            jax.ShapeDtypeStruct((1, features), jnp.float32),
            jax.ShapeDtypeStruct(cotangent.shape, jnp.bfloat16),
        ],
        scratch_shapes=[pltpu.VMEM((tokens, 1), jnp.float32)] * 2,
        compiler_params=PARAMS,
        cost_estimate=pl.CostEstimate(
            flops=8 * x.size, bytes_accessed=4 * cotangent.size + 10 * x.size, transcendentals=0
        ),
    )(*sums, cotangent, x, hidden_grad, gain_row)


def add_kernel(local_ref, received_ref, out_ref):
    out_ref[...] = (local_ref[...] + received_ref[...].astype(jnp.float32)).astype(out_ref.dtype)


def add_rows(local, received):
    height, features = received.shape
    tile = tile_of(height, 64)
    block = pl.BlockSpec((tile, features), lambda r: (r, 0))
    return pl.pallas_call(
        add_kernel,
        grid=(height // tile,),
        in_specs=[block, block],
        out_specs=block,
        out_shape=jax.ShapeDtypeStruct(local.shape, received.dtype),
        compiler_params=PARAMS,
        cost_estimate=pl.CostEstimate(flops=received.size, bytes_accessed=8 * received.size, transcendentals=0),
    )(local, received)


def weight_kernel(sources, *refs):
    cots, blocks = refs[:sources], refs[sources : 2 * sources]
    gain_ref, out_ref = refs[2 * sources], refs[-1]
    total = None
    for cot, block in zip(cots, blocks):
        term = lax.dot_general(
            cot[...], block[...], (((0,), (0,)), ((), ())), preferred_element_type=jnp.float32
        )
        total = term if total is None else total + term
    out_ref[...] = total * gain_ref[...]


def weight_columns(cots, held, received, gain_row, start, out):
    tokens, features = held[0].shape
    width = received[0].shape[1]
    rows = cots[0].shape[1]
    tile = tile_of(width, 512)
    first = start // tile
    sources = len(cots)
    whole = lambda c: (0, 0)
    placed = lambda c: (0, first + c)
    here = lambda c: (0, c)
    in_specs = [pl.BlockSpec((tokens, rows), whole)] * sources
    in_specs += [pl.BlockSpec((tokens, tile), placed)] * len(held)
    in_specs += [pl.BlockSpec((tokens, tile), here)] * len(received)
    in_specs += [pl.BlockSpec((1, tile), placed)]
    args, aliases = [*cots, *held, *received, gain_row], {}
    if out is not None:
        in_specs.append(pl.BlockSpec(memory_space=pl.ANY))
        aliases = {len(args): 0}
        args.append(out)
    return pl.pallas_call(
        functools.partial(weight_kernel, sources),
        grid=(width // tile,),
        in_specs=in_specs,
        out_specs=pl.BlockSpec((rows, tile), placed),
        out_shape=jax.ShapeDtypeStruct((rows, features), jnp.float32),
        input_output_aliases=aliases,
        compiler_params=PARAMS,
        cost_estimate=pl.CostEstimate(
            flops=2 * sources * tokens * rows * width,
            bytes_accessed=2 * sources * tokens * (rows + width) + 4 * rows * width,
            transcendentals=0,
        ),
    )(*args)


def per_device(inputs, norm_gain, value_weight, value_cotangent, upper_grad):
    replicas = Replicas("dp")
    sections = lax.axis_size("pipe")
    slices = lax.axis_size("tensor")
    x = inputs[0]
    tokens, features = x.shape
    gain_row = norm_gain
    cotangent = value_cotangent[0]
    rows = cotangent.shape[1] // replicas.count
    pair_rows = rows * replicas.width
    grad_scale = float(tokens * replicas.count) ** (-0.5)
    far = range(1, replicas.groups)
    near = range(1, replicas.width)

    down = [(i, i - 1) for i in range(1, sections)]
    upper = lax.ppermute(upper_grad[0], "pipe", down)

    columns = spans(features, Y_PARTS)

    def send_far(c, *gates):
        start, width = columns[c]
        part = (after(x, *gates) if gates else x)[:, start : start + width]
        return [replicas.send(part, high, 0) for high in far]

    far_x = [send_far(0)]
    hidden_grad, sums = hidden_grad_and_sums(cotangent, value_weight[0], x, gain_row)
    near_x = [replicas.send(after(x, sums), 0, low) for low in near]
    local, gain_grad, scaled = local_terms(
        [sums] + from_others(sums, "tensor"), cotangent, x, hidden_grad, gain_row, grad_scale
    )
    share = tokens // slices
    mine = lax.axis_index("tensor")
    own_share = lax.dynamic_slice_in_dim(scaled, mine * share, share, axis=0)
    sent = []
    for high in far:
        there = (replicas.high + high) % replicas.groups * pair_rows
        sent.append(lax.dynamic_slice_in_dim(own_share, there, pair_rows, axis=1))
    for c in range(1, len(columns)):
        far_x.append(send_far(c, *(far_x[c - 2] if c > 1 else sent)))
    pair_blocks = [lax.dynamic_slice_in_dim(scaled, replicas.high * pair_rows, pair_rows, axis=1)]
    for high, block in zip(far, sent):
        got = replicas.send(block, high, 0)
        shares = jnp.concatenate([got] + from_others(got, "tensor"), axis=0)
        pieces = [
            lax.dynamic_slice_in_dim(shares, (mine - at) % slices * share, share, axis=0) for at in range(slices)
        ]
        pair_blocks.append(jnp.concatenate(pieces, axis=0))
    pair_cot = jnp.concatenate(pair_blocks, axis=0)
    near_cots = [
        replicas.send(
            lax.dynamic_slice_in_dim(pair_cot, (replicas.low + low) % replicas.width * rows, rows, axis=1), 0, low
        )
        for low in near
    ]
    own_cot = lax.dynamic_slice_in_dim(pair_cot, replicas.low * rows, rows, axis=1)
    by_group = [own_cot] + near_cots
    blocks = [[cot[g * tokens : (g + 1) * tokens] for g in range(replicas.groups)] for cot in by_group]
    cots = [block[0] for block in blocks] + [block[high] for high in far for block in blocks]

    for others in ([(high, 0) for high in far], [(0, low) for low in near]):
        gain_grad = sum([replicas.send(gain_grad, *other) for other in others], gain_grad)

    input_grad = add_rows(local, upper)
    weight_grad = None
    for c, ((start, width), direct) in enumerate(zip(columns, far_x)):
        received = []
        for block in direct:
            gates = (input_grad, gain_grad, *near_cots) if c == len(columns) - 1 else (scaled,)
            handed = after(block, *gates)
            received += [block] + [replicas.send(handed, 0, low) for low in near]
        weight_grad = weight_columns(cots, [x] + near_x, received, gain_row, start, weight_grad)
    return (input_grad[None], weight_grad[None], gain_grad)


def solution(mesh):
    return jax.shard_map(
        per_device,
        mesh=mesh,
        in_specs=(
            P("pipe", "dp", "tensor"),
            P("pipe", "tensor"),
            P("pipe", None, "tensor"),
            P("pipe", "dp", None),
            P("pipe", "dp", "tensor"),
        ),
        out_specs=(P("pipe", "dp", "tensor"), P("pipe", "dp", "tensor"), P("pipe", "tensor")),
        check_vma=False,
    )
```

time: 85 us -> 73 us (0.86)
  the two profiles are of different devices: /device:TPU:0 before, /device:TPU:29 now
where the time goes in v2:
time: 73 us; the launch traced here: 72.5 us
  Pallas kernels  21.9 us (30%)
  starting transfers between devices  17.7 us (24%)
  local copies, waits for them, and re-layouts  15.8 us (22%)
  waiting for transfers between devices  15.6 us (21%)
  between operations  0.81 us (1%)
    ppermute x9, waiting for transfers between devices, send(): lax.ppermute(array, self.axis, [(i, self.to(i, high, low)) for i in range...  14 us
    ppermute x9, starting transfers between devices, send(): lax.ppermute(array, self.axis, [(i, self.to(i, high, low)) for i in range...  11.7 us
    unnamed x23, local copies, waits for them, and re-layouts  11.1 us
    pallas_call x2, Pallas kernels, weight_columns(): pl.pallas_call(functools.partial(weight_kernel, sources), grid=(width //...  9.97 us
    pallas_call x1, Pallas kernels, hidden_grad_and_sums(): pl.pallas_call(grad_kernel, grid=(features // tile,), in_specs=[pl.BlockS...  4.92 us
    pallas_call x1, Pallas kernels, add_rows(): pl.pallas_call(add_kernel, grid=(height // tile,), in_specs=[block, block...  3.88 us
    ppermute x1, starting transfers between devices, per_device(): upper = lax.ppermute(upper_grad[0], 'pipe', down)  3.51 us
    pallas_call x1, Pallas kernels, local_terms(): pl.pallas_call(functools.partial(local_kernel, scale, len(sums) - 1), gri...  3.1 us
  transfers between devices with their start and end apart: 12, of which 3 were waited for; matrix products, arithmetic and copies ran while one was open for 7% of the time, Pallas kernels for 24%

profile of v2, /device:TPU:29, one launch (start us, length us, event | category | flops | bytes accessed | tf_op | source)
XLA Modules:
  0.0 72.5 jit_solution(13197903875262320564)
XLA Ops:
  0.6 0.0 copy-start
  0.6 0.0 copy-start.6
  0.7 3.5 %collective-permute-start.1 = (bf16[256,4096]{1,0:T(8,128)(2,1)}, bf16[256,4096]{1,0:T(8,128)(2,1)}, u32[]{:S(2)}, u32[]{:S(2)}) collective-permute-start(bf16[256,4096]{1,0:T(8,128)(2,1)} %bitcast.18), channel_id=1, source_target_pairs={{2,0},{4,2},{6,4},{3,1},{5,3},{7,5},{10,8},{12,10},{14,12},{11,9},... | collective-permute-start | bytes 6291464 | tf_op jit(solution)/shard_map/ppermute | solution.py:255
  4.2 2.5 %slice.26 = bf16[256,2560]{1,0:T(8,128)(2,1)} slice(bf16[256,4096]{1,0:T(8,128)(2,1)} %bitcast.6), slice={[0:256], [0:2560]} | slice | bytes 2621440 | tf_op jit(solution)/shard_map/slice | solution.py:261
  6.6 0.2 collective-permute-start.10
  6.8 0.0 copy-done
  6.8 0.0 copy-done.6
  6.8 0.0 copy-start.1
  6.8 3.4 %copy-done.1 = bf16[1,1024,4096]{2,1,0:T(8,128)(2,1)S(1)} copy-done((bf16[1,1024,4096]{2,1,0:T(8,128)(2,1)S(1)}, bf16[1,1024,4096]{2,1,0:T(8,128)(2,1)}, u32[]{:S(2)}) %copy-start.1) | copy-done | bytes 8388632
  10.2 0.0 copy-start.7
  10.2 0.7 copy-done.7
  10.9 0.0 copy-start.8
  11.0 4.9 %shard_map.76 = (f32[256,4096]{1,0:T(8,128)S(1)}, f32[2,256]{1,0:T(2,128)S(1)}) custom-call(bf16[256,1024]{1,0:T(8,128)(2,1)S(1)} %bitcast.14, bf16[1024,4096]{1,0:T(8,128)(2,1)S(1)} %bitcast.13, bf16[256,4096]{1,0:T(8,128)(2,1)S(1)} %bitcast.7, f32[1,4096]{1,0:T(1,128)S(1)} %copy-done.7), custom_call_target="tpu_custom_call" | custom-call | flops 2147483648 | bytes 15204352 | tf_op jit(solution)/shard_map/pallas_call | solution.py:95
  15.9 0.0 copy-start.4
  15.9 2.0 %copy-done.4 = f32[256,4096]{1,0:T(8,128)} copy-done((f32[256,4096]{1,0:T(8,128)}, f32[256,4096]{1,0:T(8,128)S(1)}, u32[]{:S(2)}) %copy-start.4) | copy-done | bytes 4194328
  17.9 1.2 %collective-permute-start.5 = (bf16[256,4096]{1,0:T(8,128)(2,1)S(1)}, bf16[256,4096]{1,0:T(8,128)(2,1)}, u32[]{:S(2)}, u32[]{:S(2)}) collective-permute-start(bf16[256,4096]{1,0:T(8,128)(2,1)S(1)} %bitcast.8), channel_id=1, source_target_pairs={{0,8},{8,0},{16,24},{24,16},{1,9},{9,1},{17,25},{25,17},{2,10},{10... | collective-permute-start | bytes 6291464 | tf_op jit(solution)/shard_map/ppermute | solution.py:52
  19.1 1.2 %collective-permute-start = (f32[2,256]{1,0:T(2,128)S(1)}, f32[2,256]{1,0:T(2,128)S(1)}, u32[]{:S(2)}, u32[]{:S(2)}) collective-permute-start(f32[2,256]{1,0:T(2,128)S(1)} %get-tuple-element.12.refs_0_), channel_id=1, source_target_pairs={{0,1},{1,0},{2,3},{3,2},{4,5},{5,4},{6,7},{7,6},{8,9},{9,8},{10,11... | collective-permute-start | bytes 6152 | tf_op jit(solution)/shard_map/ppermute | solution.py:36
  20.3 1.6 %collective-permute-done.refs_1_ = f32[2,256]{1,0:T(2,128)S(1)} collective-permute-done((f32[2,256]{1,0:T(2,128)S(1)}, f32[2,256]{1,0:T(2,128)S(1)}, u32[]{:S(2)}, u32[]{:S(2)}) %collective-permute-start) | collective-permute-done | bytes 2080 | tf_op jit(solution)/shard_map/ppermute | solution.py:36
  22.0 0.0 copy-done.8
  22.0 0.0 copy-start.5
  22.0 2.2 %copy-done.5 = f32[256,4096]{1,0:T(8,128)S(1)} copy-done((f32[256,4096]{1,0:T(8,128)S(1)}, f32[256,4096]{1,0:T(8,128)}, u32[]{:S(2)}) %copy-start.5) | copy-done | bytes 4194328
  24.2 3.1 %shard_map.77 = (f32[256,4096]{1,0:T(8,128)S(1)}, f32[1,4096]{1,0:T(1,128)S(1)}, bf16[256,1024]{1,0:T(8,128)(2,1)S(1)}) custom-call(f32[2,256]{1,0:T(2,128)S(1)} %get-tuple-element.12.refs_0_, f32[2,256]{1,0:T(2,128)S(1)} %collective-permute-done.refs_1_, bf16[256,1024]{1,0:T(8,128)(2,1)S(1)} %bitcast.15, bf16[256,4096]{1,0:T(8,128)(2,1)S(1)} %bitcast.9, ...), custom_call_target="tpu_custom_call" | custom-call | flops 8388608 | bytes 11534336 | tf_op jit(solution)/shard_map/pallas_call | solution.py:146
  27.3 0.0 copy-start.2
  27.3 2.0 %copy-done.2 = f32[256,4096]{1,0:T(8,128)} copy-done((f32[256,4096]{1,0:T(8,128)}, f32[256,4096]{1,0:T(8,128)S(1)}, u32[]{:S(2)}) %copy-start.2) | copy-done | bytes 4194328
  29.3 0.1 dynamic_slice.20
  29.4 1.3 %collective-permute-start.2 = (bf16[128,512]{1,0:T(8,128)(2,1)S(1)}, bf16[128,512]{1,0:T(8,128)(2,1)S(1)}, u32[]{:S(2)}, u32[]{:S(2)}) collective-permute-start(bf16[128,512]{1,0:T(8,128)(2,1)S(1)} %dynamic_slice.20), channel_id=1, source_target_pairs={{0,16},{8,24},{16,0},{24,8},{1,17},{9,25},{17,1},{25,9},{2,18},{10... | collective-permute-start | bytes 393224 | tf_op jit(solution)/shard_map/ppermute | solution.py:52
  30.7 0.2 collective-permute-start.7
  30.9 8.1 %collective-permute-done.2 = bf16[128,512]{1,0:T(8,128)(2,1)S(1)} collective-permute-done((bf16[128,512]{1,0:T(8,128)(2,1)S(1)}, bf16[128,512]{1,0:T(8,128)(2,1)S(1)}, u32[]{:S(2)}, u32[]{:S(2)}) %collective-permute-start.2) | collective-permute-done | bytes 131104 | tf_op jit(solution)/shard_map/ppermute | solution.py:52
  39.1 1.2 %collective-permute-start.3 = (bf16[128,512]{1,0:T(8,128)(2,1)S(1)}, bf16[128,512]{1,0:T(8,128)(2,1)S(1)}, u32[]{:S(2)}, u32[]{:S(2)}) collective-permute-start(bf16[128,512]{1,0:T(8,128)(2,1)S(1)} %collective-permute-done.2), channel_id=1, source_target_pairs={{0,1},{1,0},{2,3},{3,2},{4,5},{5,4},{6,7},{7,6},{8,9},{9,8},{10,11... | collective-permute-start | bytes 393224 | tf_op jit(solution)/shard_map/ppermute | solution.py:36
  40.3 0.0 copy-start.3
  40.3 0.1 slice.22
  40.4 0.0 collective-permute-done.7
  40.4 0.3 collective-permute-start.6
  40.7 0.0 collective-permute-done.10.refs_6_
  40.7 2.6 %collective-permute-start.8 = (f32[1,4096]{1,0:T(1,128)S(1)}, f32[1,4096]{1,0:T(1,128)S(1)}, u32[]{:S(2)}, u32[]{:S(2)}) collective-permute-start(f32[1,4096]{1,0:T(1,128)S(1)} %add.67), channel_id=1, source_target_pairs={{0,8},{8,0},{16,24},{24,16},{1,9},{9,1},{17,25},{25,17},{2,10},{10... | collective-permute-start | bytes 49160 | tf_op jit(solution)/shard_map/ppermute | solution.py:52
  43.3 0.0 collective-permute-done.3
  43.3 2.7 %collective-permute-start.11 = (bf16[256,2560]{1,0:T(8,128)(2,1)}, bf16[256,2560]{1,0:T(8,128)(2,1)S(1)}, u32[]{:S(2)}, u32[]{:S(2)}) collective-permute-start(bf16[256,2560]{1,0:T(8,128)(2,1)} %collective-permute-done.10.refs_6_), channel_id=1, source_target_pairs={{0,8},{8,0},{16,24},{24,16},{1,9},{9,1},{17,25},{25,17},{2,10},{10... | collective-permute-start | bytes 3932168 | tf_op jit(solution)/shard_map/ppermute | solution.py:52
  46.1 0.0 copy-start.9
  46.1 0.8 %copy-done.9 = bf16[512,512]{1,0:T(8,128)(2,1)} copy-done((bf16[512,512]{1,0:T(8,128)(2,1)}, bf16[512,512]{1,0:T(8,128)(2,1)S(1)}, u32[]{:S(2)}) %copy-start.9) | copy-done | bytes 524312
  46.9 0.0 collective-permute-done.8
  46.9 0.1 collective-permute-start.4
  47.0 0.6 add.68
  47.6 0.0 collective-permute-done.1.received_ref
  47.6 0.0 copy-done.3
  47.6 3.9 %shard_map.78 = bf16[256,4096]{1,0:T(8,128)(2,1)} custom-call(f32[256,4096]{1,0:T(8,128)S(1)} %copy-done.3, bf16[256,4096]{1,0:T(8,128)(2,1)} %collective-permute-done.1.received_ref), custom_call_target="tpu_custom_call" | custom-call | flops 1048576 | bytes 8388608 | tf_op jit(solution)/shard_map/pallas_call | solution.py:182
  51.5 0.0 collective-permute-done.4
  51.5 0.0 copy-start.10
  51.5 5.9 %collective-permute-done.6.refs_6_ = bf16[256,1536]{1,0:T(8,128)(2,1)} collective-permute-done((bf16[256,1536]{1,0:T(8,128)(2,1)S(1)}, bf16[256,1536]{1,0:T(8,128)(2,1)}, u32[]{:S(2)}, u32[]{:S(2)}) %collective-permute-start.6) | collective-permute-done | bytes 786464 | tf_op jit(solution)/shard_map/ppermute | solution.py:52
  57.4 0.0 copy-done.10
  57.4 3.1 %collective-permute-start.9 = (bf16[256,1536]{1,0:T(8,128)(2,1)}, bf16[256,1536]{1,0:T(8,128)(2,1)}, u32[]{:S(2)}, u32[]{:S(2)}) collective-permute-start(bf16[256,1536]{1,0:T(8,128)(2,1)} %collective-permute-done.6.refs_6_), channel_id=1, source_target_pairs={{0,8},{8,0},{16,24},{24,16},{1,9},{9,1},{17,25},{25,17},{2,10},{10... | collective-permute-start | bytes 2359304 | tf_op jit(solution)/shard_map/ppermute | solution.py:52
  60.5 1.0 %fusion = (bf16[256,256]{1,0:T(8,128)(2,1)S(1)}, bf16[256,256]{1,0:T(8,128)(2,1)S(1)}) fusion(bf16[512,512]{1,0:T(8,128)(2,1)} %copy-done.9, s32[]{:T(128)S(6)} %add.69, s32[]{:T(128)S(6)} %select_n.64), kind=kLoop, calls=%fused_computation.8 | loop fusion | bytes 524296 | tf_op jit(solution)/shard_map/slice | solution.py:296
  61.5 1.0 %fusion.1 = (bf16[256,256]{1,0:T(8,128)(2,1)S(1)}, bf16[256,256]{1,0:T(8,128)(2,1)S(1)}) fusion(bf16[512,256]{1,0:T(8,128)(2,1)} %copy-done.10), kind=kLoop, calls=%fused_computation.9 | loop fusion | bytes 524288 | tf_op jit(solution)/shard_map/slice | solution.py:296
  62.5 0.0 collective-permute-done.5.refs_5_
  62.5 0.0 collective-permute-done.11.refs_7_
  62.5 5.8 %shard_map.79.refs_9_ = f32[256,4096]{1,0:T(8,128)} custom-call(bf16[256,256]{1,0:T(8,128)(2,1)S(1)} %get-tuple-element.22.refs_0_, bf16[256,256]{1,0:T(8,128)(2,1)S(1)} %get-tuple-element.24.refs_1_, bf16[256,256]{1,0:T(8,128)(2,1)S(1)} %get-tuple-element.21.refs_2_, bf16[256,256]{1,0:T(8,128)(2,1)S(1)} %get-tuple-element.23.refs_3_, ...), custom_call_target="tpu_custom_call" | custom-call | flops 1342177280 | bytes 8388608 | tf_op jit(solution)/shard_map/pallas_call | solution.py:224
  68.3 0.0 collective-permute-done.9.refs_7_
  68.3 4.2 %shard_map.80 = f32[256,4096]{1,0:T(8,128)} custom-call(bf16[256,256]{1,0:T(8,128)(2,1)S(1)} %get-tuple-element.22.refs_0_, bf16[256,256]{1,0:T(8,128)(2,1)S(1)} %get-tuple-element.24.refs_1_, bf16[256,256]{1,0:T(8,128)(2,1)S(1)} %get-tuple-element.21.refs_2_, bf16[256,256]{1,0:T(8,128)(2,1)S(1)} %get-tuple-element.23.refs_3_, ...), custom_call_target="tpu_custom_call", output_to_operand_aliasing={{}: (9, {})} | custom-call | flops 805306368 | bytes 5242880 | tf_op jit(solution)/shard_map/pallas_call | solution.py:224
  (7 shorter events, 0.1 us)
Async XLA Ops:
  0.6 6.2 %copy-start = (bf16[1,256,4096]{2,1,0:T(8,128)(2,1)S(1)}, bf16[1,256,4096]{2,1,0:T(8,128)(2,1)}, u32[]{:S(2)}) copy-start(bf16[1,256,4096]{2,1,0:T(8,128)(2,1)} %param.5) | copy-start | bytes 6291460
  0.6 6.2 %copy-start.6 = (bf16[1,256,1024]{2,1,0:T(8,128)(2,1)S(1)}, bf16[1,256,1024]{2,1,0:T(8,128)(2,1)}, u32[]{:S(2)}) copy-start(bf16[1,256,1024]{2,1,0:T(8,128)(2,1)} %param.8) | copy-start | bytes 1572868
  0.7 47.0 %collective-permute-start.1 = (bf16[256,4096]{1,0:T(8,128)(2,1)}, bf16[256,4096]{1,0:T(8,128)(2,1)}, u32[]{:S(2)}, u32[]{:S(2)}) collective-permute-start(bf16[256,4096]{1,0:T(8,128)(2,1)} %bitcast.18), channel_id=1, source_target_pairs={{2,0},{4,2},{6,4},{3,1},{5,3},{7,5},{10,8},{12,10},{14,12},{11,9},... | collective-permute-start | bytes 6291464 | tf_op jit(solution)/shard_map/ppermute | solution.py:255
  6.6 34.1 %collective-permute-start.10 = (bf16[256,2560]{1,0:T(8,128)(2,1)}, bf16[256,2560]{1,0:T(8,128)(2,1)}, u32[]{:S(2)}, u32[]{:S(2)}) collective-permute-start(bf16[256,2560]{1,0:T(8,128)(2,1)} %slice.26), channel_id=1, source_target_pairs={{0,16},{8,24},{16,0},{24,8},{1,17},{9,25},{17,1},{25,9},{2,18},{10... | collective-permute-start | bytes 3932168 | tf_op jit(solution)/shard_map/ppermute | solution.py:52
  6.8 3.4 %copy-start.1 = (bf16[1,1024,4096]{2,1,0:T(8,128)(2,1)S(1)}, bf16[1,1024,4096]{2,1,0:T(8,128)(2,1)}, u32[]{:S(2)}) copy-start(bf16[1,1024,4096]{2,1,0:T(8,128)(2,1)} %param.7) | copy-start | bytes 25165828
  10.2 0.7 copy-start.7
  10.9 11.0 %copy-start.8 = (f32[1,4096]{1,0:T(1,128)S(1)}, f32[1,4096]{1,0:T(1,128)}, u32[]{:S(2)}) copy-start(f32[1,4096]{1,0:T(1,128)} %refs_8_.3) | copy-start | bytes 49156
  15.9 2.0 %copy-start.4 = (f32[256,4096]{1,0:T(8,128)}, f32[256,4096]{1,0:T(8,128)S(1)}, u32[]{:S(2)}) copy-start(f32[256,4096]{1,0:T(8,128)S(1)} %get-tuple-element.13.refs_4_) | copy-start | bytes 12582916
  17.9 44.6 %collective-permute-start.5 = (bf16[256,4096]{1,0:T(8,128)(2,1)S(1)}, bf16[256,4096]{1,0:T(8,128)(2,1)}, u32[]{:S(2)}, u32[]{:S(2)}) collective-permute-start(bf16[256,4096]{1,0:T(8,128)(2,1)S(1)} %bitcast.8), channel_id=1, source_target_pairs={{0,8},{8,0},{16,24},{24,16},{1,9},{9,1},{17,25},{25,17},{2,10},{10... | collective-permute-start | bytes 6291464 | tf_op jit(solution)/shard_map/ppermute | solution.py:52
  19.1 2.8 %collective-permute-start = (f32[2,256]{1,0:T(2,128)S(1)}, f32[2,256]{1,0:T(2,128)S(1)}, u32[]{:S(2)}, u32[]{:S(2)}) collective-permute-start(f32[2,256]{1,0:T(2,128)S(1)} %get-tuple-element.12.refs_0_), channel_id=1, source_target_pairs={{0,1},{1,0},{2,3},{3,2},{4,5},{5,4},{6,7},{7,6},{8,9},{9,8},{10,11... | collective-permute-start | bytes 6152 | tf_op jit(solution)/shard_map/ppermute | solution.py:36
  22.0 2.2 %copy-start.5 = (f32[256,4096]{1,0:T(8,128)S(1)}, f32[256,4096]{1,0:T(8,128)}, u32[]{:S(2)}) copy-start(f32[256,4096]{1,0:T(8,128)} %copy-done.4) | copy-start | bytes 12582916
  27.3 2.0 %copy-start.2 = (f32[256,4096]{1,0:T(8,128)}, f32[256,4096]{1,0:T(8,128)S(1)}, u32[]{:S(2)}) copy-start(f32[256,4096]{1,0:T(8,128)S(1)} %get-tuple-element.14.local_ref) | copy-start | bytes 12582916
  29.4 9.7 %collective-permute-start.2 = (bf16[128,512]{1,0:T(8,128)(2,1)S(1)}, bf16[128,512]{1,0:T(8,128)(2,1)S(1)}, u32[]{:S(2)}, u32[]{:S(2)}) collective-permute-start(bf16[128,512]{1,0:T(8,128)(2,1)S(1)} %dynamic_slice.20), channel_id=1, source_target_pairs={{0,16},{8,24},{16,0},{24,8},{1,17},{9,25},{17,1},{25,9},{2,18},{10... | collective-permute-start | bytes 393224 | tf_op jit(solution)/shard_map/ppermute | solution.py:52
  30.7 9.7 %collective-permute-start.7 = (f32[1,4096]{1,0:T(1,128)S(1)}, f32[1,4096]{1,0:T(1,128)S(1)}, u32[]{:S(2)}, u32[]{:S(2)}) collective-permute-start(f32[1,4096]{1,0:T(1,128)S(1)} %get-tuple-element.18), channel_id=1, source_target_pairs={{0,16},{8,24},{16,0},{24,8},{1,17},{9,25},{17,1},{25,9},{2,18},{10... | collective-permute-start | bytes 49160 | tf_op jit(solution)/shard_map/ppermute | solution.py:52
  39.1 4.2 %collective-permute-start.3 = (bf16[128,512]{1,0:T(8,128)(2,1)S(1)}, bf16[128,512]{1,0:T(8,128)(2,1)S(1)}, u32[]{:S(2)}, u32[]{:S(2)}) collective-permute-start(bf16[128,512]{1,0:T(8,128)(2,1)S(1)} %collective-permute-done.2), channel_id=1, source_target_pairs={{0,1},{1,0},{2,3},{3,2},{4,5},{5,4},{6,7},{7,6},{8,9},{9,8},{10,11... | collective-permute-start | bytes 393224 | tf_op jit(solution)/shard_map/ppermute | solution.py:36
  40.3 7.3 %copy-start.3 = (f32[256,4096]{1,0:T(8,128)S(1)}, f32[256,4096]{1,0:T(8,128)}, u32[]{:S(2)}) copy-start(f32[256,4096]{1,0:T(8,128)} %copy-done.2) | copy-start | bytes 12582916
  40.4 17.0 %collective-permute-start.6 = (bf16[256,1536]{1,0:T(8,128)(2,1)S(1)}, bf16[256,1536]{1,0:T(8,128)(2,1)}, u32[]{:S(2)}, u32[]{:S(2)}) collective-permute-start(bf16[256,1536]{1,0:T(8,128)(2,1)S(1)} %slice.22), channel_id=1, source_target_pairs={{0,16},{8,24},{16,0},{24,8},{1,17},{9,25},{17,1},{25,9},{2,18},{10... | collective-permute-start | bytes 2359304 | tf_op jit(solution)/shard_map/ppermute | solution.py:52
  40.7 6.2 %collective-permute-start.8 = (f32[1,4096]{1,0:T(1,128)S(1)}, f32[1,4096]{1,0:T(1,128)S(1)}, u32[]{:S(2)}, u32[]{:S(2)}) collective-permute-start(f32[1,4096]{1,0:T(1,128)S(1)} %add.67), channel_id=1, source_target_pairs={{0,8},{8,0},{16,24},{24,16},{1,9},{9,1},{17,25},{25,17},{2,10},{10... | collective-permute-start | bytes 49160 | tf_op jit(solution)/shard_map/ppermute | solution.py:52
  43.3 19.2 %collective-permute-start.11 = (bf16[256,2560]{1,0:T(8,128)(2,1)}, bf16[256,2560]{1,0:T(8,128)(2,1)S(1)}, u32[]{:S(2)}, u32[]{:S(2)}) collective-permute-start(bf16[256,2560]{1,0:T(8,128)(2,1)} %collective-permute-done.10.refs_6_), channel_id=1, source_target_pairs={{0,8},{8,0},{16,24},{24,16},{1,9},{9,1},{17,25},{25,17},{2,10},{10... | collective-permute-start | bytes 3932168 | tf_op jit(solution)/shard_map/ppermute | solution.py:52
  46.1 0.8 %copy-start.9 = (bf16[512,512]{1,0:T(8,128)(2,1)}, bf16[512,512]{1,0:T(8,128)(2,1)S(1)}, u32[]{:S(2)}) copy-start(bf16[512,512]{1,0:T(8,128)(2,1)S(1)} %pad_maximum_fusion) | copy-start | bytes 1572868
  46.9 4.6 %collective-permute-start.4 = (bf16[512,256]{1,0:T(8,128)(2,1)S(1)}, bf16[512,256]{1,0:T(8,128)(2,1)S(1)}, u32[]{:S(2)}, u32[]{:S(2)}) collective-permute-start(bf16[512,256]{1,0:T(8,128)(2,1)S(1)} %constant_dynamic-slice_fusion.1), channel_id=1, source_target_pairs={{0,8},{8,0},{16,24},{24,16},{1,9},{9,1},{17,25},{25,17},{2,10},{10... | collective-permute-start | bytes 786440 | tf_op jit(solution)/shard_map/ppermute | solution.py:52
  51.5 5.9 %copy-start.10 = (bf16[512,256]{1,0:T(8,128)(2,1)}, bf16[512,256]{1,0:T(8,128)(2,1)S(1)}, u32[]{:S(2)}) copy-start(bf16[512,256]{1,0:T(8,128)(2,1)S(1)} %collective-permute-done.4) | copy-start | bytes 786436
  57.4 10.9 %collective-permute-start.9 = (bf16[256,1536]{1,0:T(8,128)(2,1)}, bf16[256,1536]{1,0:T(8,128)(2,1)}, u32[]{:S(2)}, u32[]{:S(2)}) collective-permute-start(bf16[256,1536]{1,0:T(8,128)(2,1)} %collective-permute-done.6.refs_6_), channel_id=1, source_target_pairs={{0,8},{8,0},{16,24},{24,16},{1,9},{9,1},{17,25},{25,17},{2,10},{10... | collective-permute-start | bytes 2359304 | tf_op jit(solution)/shard_map/ppermute | solution.py:52

commit v3 on v2

--- a/solution.py
+++ b/solution.py
@@ -9,9 +9,10 @@
 
 D = 8192
 EPS = 1e-05
-Y_PARTS = (5, 3)
+Y_PARTS = (1, 1)
 MIB = 1 << 20
 PARAMS = pltpu.CompilerParams(vmem_limit_bytes=24 * MIB)
+STREAMED = pltpu.CompilerParams(vmem_limit_bytes=56 * MIB)
 
 
 def after(value, *others):
@@ -42,11 +43,12 @@
         self.count = lax.axis_size(axis)
         self.width = 2 if self.count % 2 == 0 else 1
         self.groups = self.count // self.width
-        self.high = lax.axis_index(axis) // self.width
-        self.low = lax.axis_index(axis) % self.width
 
     def to(self, index, high, low):
         return (index // self.width + high) % self.groups * self.width + (index % self.width + low) % self.width
+
+    def index(self, high, low):
+        return self.to(lax.axis_index(self.axis), high, low)
 
     def send(self, array, high, low):
         return lax.ppermute(array, self.axis, [(i, self.to(i, high, low)) for i in range(self.count)])
@@ -107,7 +109,7 @@
             jax.ShapeDtypeStruct((2, tokens), jnp.float32),
         ],
         scratch_shapes=[pltpu.VMEM((tokens, 128), jnp.float32)] * 2,
-        compiler_params=PARAMS,
+        compiler_params=STREAMED,
         cost_estimate=pl.CostEstimate(
             flops=2 * tokens * features * weight.shape[0],
             bytes_accessed=2 * (weight.size + cotangent.size + x.size) + 4 * x.size,
@@ -130,7 +132,7 @@
         center_row = inverse_row * sums[1:2] / D
         inverse[...] = row_to_column(inverse_row)
         factor[...] = row_to_column(inverse_row * center_row)
-        scaled_ref[...] = (cot_ref[...].astype(jnp.float32) * (inverse[...] * scale)).astype(jnp.bfloat16)
+        scaled_ref[...] = (cot_ref[...].astype(jnp.float32).T * (inverse_row * scale)).astype(jnp.bfloat16)
 
     x = x_ref[...].astype(jnp.float32)
     hidden_grad = hidden_grad_ref[...]
@@ -156,28 +158,51 @@
         out_specs=[
             pl.BlockSpec((tokens, tile), column),
             pl.BlockSpec((1, tile), column),
-            pl.BlockSpec(cotangent.shape, whole),
+            pl.BlockSpec(cotangent.shape[::-1], whole),
         ],
         out_shape=[
             jax.ShapeDtypeStruct((tokens, features), jnp.float32),
             jax.ShapeDtypeStruct((1, features), jnp.float32),
-            jax.ShapeDtypeStruct(cotangent.shape, jnp.bfloat16),
+            jax.ShapeDtypeStruct(cotangent.shape[::-1], jnp.bfloat16),
         ],
         scratch_shapes=[pltpu.VMEM((tokens, 1), jnp.float32)] * 2,
-        compiler_params=PARAMS,
+        compiler_params=STREAMED,
         cost_estimate=pl.CostEstimate(
             flops=8 * x.size, bytes_accessed=4 * cotangent.size + 10 * x.size, transcendentals=0
         ),
     )(*sums, cotangent, x, hidden_grad, gain_row)
 
 
+def split_kernel(columns, x_ref, *refs):
+    parts, sems = refs[:-1], refs[-1]
+    copies = [
+        pltpu.make_async_copy(x_ref.at[:, start : start + width], part, sems.at[at])
+        for at, ((start, width), part) in enumerate(zip(columns, parts))
+    ]
+    for copy in copies:
+        copy.start()
+    for copy in copies:
+        copy.wait()
+
+
+def split_columns(x, columns):
+    return pl.pallas_call(
+        functools.partial(split_kernel, columns),
+        in_specs=[pl.BlockSpec(memory_space=pl.ANY)],
+        out_specs=[pl.BlockSpec(memory_space=pl.ANY)] * len(columns),
+        out_shape=[jax.ShapeDtypeStruct((x.shape[0], width), x.dtype) for _, width in columns],
+        scratch_shapes=[pltpu.SemaphoreType.DMA((len(columns),))],
+        cost_estimate=pl.CostEstimate(flops=0, bytes_accessed=4 * x.size, transcendentals=0),
+    )(x)
+
+
 def add_kernel(local_ref, received_ref, out_ref):
     out_ref[...] = (local_ref[...] + received_ref[...].astype(jnp.float32)).astype(out_ref.dtype)
 
 
 def add_rows(local, received):
     height, features = received.shape
-    tile = tile_of(height, 64)
+    tile = tile_of(height, 32)
     block = pl.BlockSpec((tile, features), lambda r: (r, 0))
     return pl.pallas_call(
         add_kernel,
@@ -190,39 +215,38 @@
     )(local, received)
 
 
-def weight_kernel(sources, *refs):
-    cots, blocks = refs[:sources], refs[sources : 2 * sources]
-    gain_ref, out_ref = refs[2 * sources], refs[-1]
+def weight_kernel(groups, *refs):
+    scaled_refs, gain_ref, blocks, out_ref = refs[:groups], refs[groups], refs[groups + 1 :], refs[-1]
+    tokens = blocks[0].shape[0]
+    width = scaled_refs[0].shape[1] // tokens
     total = None
-    for cot, block in zip(cots, blocks):
-        term = lax.dot_general(
-            cot[...], block[...], (((0,), (0,)), ((), ())), preferred_element_type=jnp.float32
-        )
+    for at in range(groups * width):
+        scaled = scaled_refs[at // width][:, at % width * tokens : (at % width + 1) * tokens]
+        term = jnp.dot(scaled, blocks[at][...], preferred_element_type=jnp.float32)
         total = term if total is None else total + term
     out_ref[...] = total * gain_ref[...]
 
 
-def weight_columns(cots, held, received, gain_row, start, out):
+def weight_columns(scaled, held, received, gain_row, start, out):
     tokens, features = held[0].shape
     width = received[0].shape[1]
-    rows = cots[0].shape[1]
+    rows = scaled[0].shape[0]
     tile = tile_of(width, 512)
     first = start // tile
-    sources = len(cots)
     whole = lambda c: (0, 0)
     placed = lambda c: (0, first + c)
     here = lambda c: (0, c)
-    in_specs = [pl.BlockSpec((tokens, rows), whole)] * sources
+    in_specs = [pl.BlockSpec(part.shape, whole) for part in scaled] + [pl.BlockSpec((1, tile), placed)]
     in_specs += [pl.BlockSpec((tokens, tile), placed)] * len(held)
     in_specs += [pl.BlockSpec((tokens, tile), here)] * len(received)
-    in_specs += [pl.BlockSpec((1, tile), placed)]
-    args, aliases = [*cots, *held, *received, gain_row], {}
+    args, aliases = [*scaled, gain_row, *held, *received], {}
     if out is not None:
         in_specs.append(pl.BlockSpec(memory_space=pl.ANY))
         aliases = {len(args): 0}
         args.append(out)
-    return pl.pallas_call(
-        functools.partial(weight_kernel, sources),
+    sources = len(held) + len(received)
+    return pl.pallas_call(
+        functools.partial(weight_kernel, len(scaled)),
         grid=(width // tile,),
         in_specs=in_specs,
         out_specs=pl.BlockSpec((rows, tile), placed),
@@ -246,67 +270,60 @@
     gain_row = norm_gain
     cotangent = value_cotangent[0]
     rows = cotangent.shape[1] // replicas.count
-    pair_rows = rows * replicas.width
     grad_scale = float(tokens * replicas.count) ** (-0.5)
     far = range(1, replicas.groups)
     near = range(1, replicas.width)
 
+    columns = spans(features, Y_PARTS)
+    parts = split_columns(x, columns)
+    far_x = [[replicas.send(parts[0], high, 0) for high in far]]
     down = [(i, i - 1) for i in range(1, sections)]
-    upper = lax.ppermute(upper_grad[0], "pipe", down)
-
-    columns = spans(features, Y_PARTS)
-
-    def send_far(c, *gates):
-        start, width = columns[c]
-        part = (after(x, *gates) if gates else x)[:, start : start + width]
-        return [replicas.send(part, high, 0) for high in far]
-
-    far_x = [send_far(0)]
+    upper = lax.ppermute(after(upper_grad[0], parts[0]), "pipe", down)
+
     hidden_grad, sums = hidden_grad_and_sums(cotangent, value_weight[0], x, gain_row)
     near_x = [replicas.send(after(x, sums), 0, low) for low in near]
     local, gain_grad, scaled = local_terms(
         [sums] + from_others(sums, "tensor"), cotangent, x, hidden_grad, gain_row, grad_scale
     )
-    share = tokens // slices
+
+    by_core = scaled.reshape(replicas.count, rows, tokens)
+    turn = replicas.width - 1
+    rows_for = lambda high, low: lax.dynamic_index_in_dim(by_core, replicas.index(high, low), 0, False)
+    pair = [[rows_for(high, turn if high else 0)] for high in range(replicas.groups)]
+    for low in near:
+        theirs = jnp.stack([rows_for(high, turn + low if high else low) for high in range(replicas.groups)])
+        swapped = replicas.send(theirs, 0, low)
+        for high in range(replicas.groups):
+            pair[high].append(swapped[high])
+    pair = [jnp.concatenate(blocks, axis=1) for blocks in pair]
+    cots = [pair[0]]
+    share = tokens * replicas.width // slices
     mine = lax.axis_index("tensor")
-    own_share = lax.dynamic_slice_in_dim(scaled, mine * share, share, axis=0)
-    sent = []
-    for high in far:
-        there = (replicas.high + high) % replicas.groups * pair_rows
-        sent.append(lax.dynamic_slice_in_dim(own_share, there, pair_rows, axis=1))
-    for c in range(1, len(columns)):
-        far_x.append(send_far(c, *(far_x[c - 2] if c > 1 else sent)))
-    pair_blocks = [lax.dynamic_slice_in_dim(scaled, replicas.high * pair_rows, pair_rows, axis=1)]
-    for high, block in zip(far, sent):
-        got = replicas.send(block, high, 0)
-        shares = jnp.concatenate([got] + from_others(got, "tensor"), axis=0)
+    got = [
+        replicas.send(lax.dynamic_slice_in_dim(pair[high], mine * share, share, axis=1), high, turn) for high in far
+    ]
+    for block in got:
+        shares = jnp.concatenate([block] + from_others(block, "tensor"), axis=1)
         pieces = [
-            lax.dynamic_slice_in_dim(shares, (mine - at) % slices * share, share, axis=0) for at in range(slices)
+            lax.dynamic_slice_in_dim(shares, (mine - at) % slices * share, share, axis=1) for at in range(slices)
         ]
-        pair_blocks.append(jnp.concatenate(pieces, axis=0))
-    pair_cot = jnp.concatenate(pair_blocks, axis=0)
-    near_cots = [
-        replicas.send(
-            lax.dynamic_slice_in_dim(pair_cot, (replicas.low + low) % replicas.width * rows, rows, axis=1), 0, low
-        )
-        for low in near
-    ]
-    own_cot = lax.dynamic_slice_in_dim(pair_cot, replicas.low * rows, rows, axis=1)
-    by_group = [own_cot] + near_cots
-    blocks = [[cot[g * tokens : (g + 1) * tokens] for g in range(replicas.groups)] for cot in by_group]
-    cots = [block[0] for block in blocks] + [block[high] for high in far for block in blocks]
-
-    for others in ([(high, 0) for high in far], [(0, low) for low in near]):
-        gain_grad = sum([replicas.send(gain_grad, *other) for other in others], gain_grad)
-
-    input_grad = add_rows(local, upper)
+        cots.append(jnp.concatenate(pieces, axis=1))
+    gain_far = [replicas.send(gain_grad, high, turn) for high in far]
+    gain_grad = sum(gain_far, gain_grad)
+
+    far_x += [[replicas.send(after(part, *got, *gain_far), high, 0) for high in far] for part in parts[1:]]
     weight_grad = None
     for c, ((start, width), direct) in enumerate(zip(columns, far_x)):
+        gates = got + gain_far
+        if c == len(columns) - 1:
+            input_grad = add_rows(local, upper)
+            gated = after(gain_grad, input_grad)
+            gain_grad = sum([replicas.send(gated, 0, low) for low in near], gated)
+            gates = [gain_grad] + [w for w in [weight_grad] if w is not None]
         received = []
         for block in direct:
-            gates = (input_grad, gain_grad, *near_cots) if c == len(columns) - 1 else (scaled,)
-            handed = after(block, *gates)
-            received += [block] + [replicas.send(handed, 0, low) for low in near]
+            handed = after(block, *gates) if gates else block
+            received += [replicas.send(handed, 0, low) for low in near] + [block]
         weight_grad = weight_columns(cots, [x] + near_x, received, gain_row, start, weight_grad)
     return (input_grad[None], weight_grad[None], gain_grad)
 

time: 73 us -> 139 us (1.90)
  the two profiles are of different devices: /device:TPU:29 before, /device:TPU:0 now
where the time goes in v3:
time: 139 us; the launch traced here: 138 us
  Pallas kernels  98.3 us (71%)
  waiting for transfers between devices  22.9 us (16%)
  starting transfers between devices  10.9 us (8%)
  local copies, waits for them, and re-layouts  3.99 us (3%)
  other arithmetic  1.49 us (1%)
    pallas_call x1, Pallas kernels, split_columns(): pl.pallas_call(functools.partial(split_kernel, columns), in_specs=[pl.Blo...  64.7 us
    pallas_call x1, Pallas kernels, hidden_grad_and_sums(): pl.pallas_call(grad_kernel, grid=(features // tile,), in_specs=[pl.BlockS...  10.1 us
    ppermute x1, waiting for transfers between devices, per_device(): upper = lax.ppermute(after(upper_grad[0], parts[0]), 'pipe', down)  9.36 us
    pallas_call x2, Pallas kernels, weight_columns(): pl.pallas_call(functools.partial(weight_kernel, len(scaled)), grid=(width...  9.21 us
    pallas_call x1, Pallas kernels, local_terms(): pl.pallas_call(functools.partial(local_kernel, scale, len(sums) - 1), gri...  8.49 us
    ppermute x9, waiting for transfers between devices, send(): lax.ppermute(array, self.axis, [(i, self.to(i, high, low)) for i in range...  7.9 us
    ppermute x9, starting transfers between devices, send(): lax.ppermute(array, self.axis, [(i, self.to(i, high, low)) for i in range...  6.03 us
    pallas_call x1, Pallas kernels, add_rows(): pl.pallas_call(add_kernel, grid=(height // tile,), in_specs=[block, block...  5.88 us
  transfers between devices with their start and end apart: 12, of which 6 were waited for; matrix products, arithmetic and copies ran while one was open for 2% of the time, Pallas kernels for 21%

profile of v3, /device:TPU:0, one launch (start us, length us, event | category | flops | bytes accessed | tf_op | source)
XLA Modules:
  0.0 138.4 jit_solution(17674482264442659314)
XLA Ops:
  0.6 64.7 %shard_map.78 = (bf16[256,2048]{1,0:T(8,128)(2,1)}, bf16[256,2048]{1,0:T(8,128)(2,1)}) custom-call(bf16[256,4096]{1,0:T(8,128)(2,1)} %bitcast.15), custom_call_target="tpu_custom_call" | custom-call | bytes 4194304 | tf_op jit(solution)/shard_map/pallas_call | solution.py:189
  65.3 3.0 %collective-permute-start.9 = (bf16[256,2048]{1,0:T(8,128)(2,1)}, bf16[256,2048]{1,0:T(8,128)(2,1)}, u32[]{:S(2)}, u32[]{:S(2)}) collective-permute-start(bf16[256,2048]{1,0:T(8,128)(2,1)} %get-tuple-element.19), channel_id=1, source_target_pairs={{0,16},{8,24},{16,0},{24,8},{1,17},{9,25},{17,1},{25,9},{2,18},{10... | collective-permute-start | bytes 3145736 | tf_op jit(solution)/shard_map/ppermute | solution.py:54
  68.3 1.3 collective-permute-start.1
  69.6 0.0 copy-start
  69.6 10.1 %shard_map.76 = (f32[256,4096]{1,0:T(8,128)}, f32[2,256]{1,0:T(2,128)}) custom-call(bf16[256,1024]{1,0:T(8,128)(2,1)} %bitcast.24, bf16[1024,4096]{1,0:T(8,128)(2,1)} %bitcast.22, bf16[256,4096]{1,0:T(8,128)(2,1)} %bitcast.16, f32[1,4096]{1,0:T(1,128)} %refs_2_.3), custom_call_target="tpu_custom_call" | custom-call | flops 2147483648 | bytes 15204352 | tf_op jit(solution)/shard_map/pallas_call | solution.py:97
  79.7 0.0 copy-done
  79.7 0.0 collective-permute-start.5
  79.7 1.6 %collective-permute-start = (f32[2,256]{1,0:T(2,128)}, f32[2,256]{1,0:T(2,128)S(1)}, u32[]{:S(2)}, u32[]{:S(2)}) collective-permute-start(f32[2,256]{1,0:T(2,128)} %get-tuple-element.16.refs_0_), channel_id=1, source_target_pairs={{0,1},{1,0},{2,3},{3,2},{4,5},{5,4},{6,7},{7,6},{8,9},{9,8},{10,11... | collective-permute-start | bytes 6152 | tf_op jit(solution)/shard_map/ppermute | solution.py:37
  81.3 2.2 %collective-permute-done.refs_1_ = f32[2,256]{1,0:T(2,128)S(1)} collective-permute-done((f32[2,256]{1,0:T(2,128)}, f32[2,256]{1,0:T(2,128)S(1)}, u32[]{:S(2)}, u32[]{:S(2)}) %collective-permute-start) | collective-permute-done | bytes 2080 | tf_op jit(solution)/shard_map/ppermute | solution.py:37
  83.5 0.0 copy-start.4
  83.5 0.6 copy-done.4
  84.0 8.5 %shard_map.77 = (f32[256,4096]{1,0:T(8,128)}, f32[1,4096]{1,0:T(1,128)}, bf16[1024,256]{1,0:T(8,128)(2,1)}) custom-call(f32[2,256]{1,0:T(2,128)} %get-tuple-element.16.refs_0_, f32[2,256]{1,0:T(2,128)} %copy-done.4, bf16[256,1024]{1,0:T(8,128)(2,1)} %bitcast.25, bf16[256,4096]{1,0:T(8,128)(2,1)} %bitcast.17, f32[256,4096]{1,0:T(8,128)} %get-tuple-element.17.refs_4_, ...), custom_call_target="tpu_custom_call" | custom-call | flops 8388608 | bytes 11534336 | tf_op jit(solution)/shard_map/pallas_call | solution.py:148
  92.5 1.1 dynamic-slice_bitcast_fusion
  93.7 0.1 collective-permute-start.2
  93.8 1.5 %collective-permute-done.2 = bf16[2,256,256]{2,1,0:T(8,128)(2,1)S(1)} collective-permute-done((bf16[2,256,256]{2,1,0:T(8,128)(2,1)S(1)}, bf16[2,256,256]{2,1,0:T(8,128)(2,1)S(1)}, u32[]{:S(2)}, u32[]{:S(2)}) %collective-permute-start.2) | collective-permute-done | bytes 262176 | tf_op jit(solution)/shard_map/ppermute | solution.py:54
  95.3 0.1 fusion
  95.4 0.1 collective-permute-start.3
  95.5 1.7 %collective-permute-start.6 = (f32[1,4096]{1,0:T(1,128)}, f32[1,4096]{1,0:T(1,128)S(1)}, u32[]{:S(2)}, u32[]{:S(2)}) collective-permute-start(f32[1,4096]{1,0:T(1,128)} %get-tuple-element.24), channel_id=1, source_target_pairs={{0,24},{8,16},{16,8},{24,0},{1,25},{9,17},{17,9},{25,1},{2,26},{10... | collective-permute-start | bytes 49160 | tf_op jit(solution)/shard_map/ppermute | solution.py:54
  97.2 4.1 %collective-permute-done.6 = f32[1,4096]{1,0:T(1,128)S(1)} collective-permute-done((f32[1,4096]{1,0:T(1,128)}, f32[1,4096]{1,0:T(1,128)S(1)}, u32[]{:S(2)}, u32[]{:S(2)}) %collective-permute-start.6) | collective-permute-done | bytes 16416 | tf_op jit(solution)/shard_map/ppermute | solution.py:54
  101.3 0.0 collective-permute-done.3
  101.3 0.0 collective-permute-done.9.refs_6_
  101.3 0.5 collective-permute-start.10
  101.8 0.0 collective-permute-start.7
  101.9 0.7 add.106
  102.6 2.0 %collective-permute-start.4 = (bf16[256,256]{1,0:T(8,128)(2,1)S(1)}, bf16[256,256]{1,0:T(8,128)(2,1)S(1)}, u32[]{:S(2)}, u32[]{:S(2)}) collective-permute-start(bf16[256,256]{1,0:T(8,128)(2,1)S(1)} %collective-permute-done.3), channel_id=1, source_target_pairs={{0,1},{1,0},{2,3},{3,2},{4,5},{5,4},{6,7},{7,6},{8,9},{9,8},{10,11... | collective-permute-start | bytes 393224 | tf_op jit(solution)/shard_map/ppermute | solution.py:37
  104.7 3.5 %collective-permute-done.4 = bf16[256,256]{1,0:T(8,128)(2,1)S(1)} collective-permute-done((bf16[256,256]{1,0:T(8,128)(2,1)S(1)}, bf16[256,256]{1,0:T(8,128)(2,1)S(1)}, u32[]{:S(2)}, u32[]{:S(2)}) %collective-permute-start.4) | collective-permute-done | bytes 131104 | tf_op jit(solution)/shard_map/ppermute | solution.py:37
  108.3 9.4 %collective-permute-done.1.received_ref = bf16[256,4096]{1,0:T(8,128)(2,1)} collective-permute-done((bf16[256,4096]{1,0:T(8,128)(2,1)}, bf16[256,4096]{1,0:T(8,128)(2,1)}, u32[]{:S(2)}, u32[]{:S(2)}) %collective-permute-start.1) | collective-permute-done | bytes 2097184 | tf_op jit(solution)/shard_map/ppermute | solution.py:281
  117.6 0.0 copy-start.2
  117.6 2.2 %copy-done.2 = f32[256,4096]{1,0:T(8,128)S(1)} copy-done((f32[256,4096]{1,0:T(8,128)S(1)}, f32[256,4096]{1,0:T(8,128)}, u32[]{:S(2)}) %copy-start.2) | copy-done | bytes 4194328
  119.8 0.0 copy-start.1
  119.8 0.0 copy-start.3
  119.8 5.9 %shard_map.79 = bf16[256,4096]{1,0:T(8,128)(2,1)} custom-call(f32[256,4096]{1,0:T(8,128)S(1)} %copy-done.2, bf16[256,4096]{1,0:T(8,128)(2,1)} %collective-permute-done.1.received_ref), custom_call_target="tpu_custom_call" | custom-call | flops 1048576 | bytes 8388608 | tf_op jit(solution)/shard_map/pallas_call | solution.py:207
  125.7 0.0 collective-permute-start.8
  125.7 0.0 collective-permute-done.10.refs_5_
  125.7 0.0 collective-permute-done.5.refs_4_
  125.7 0.0 copy-done.1
  125.7 0.0 copy-done.3
  125.7 4.8 %shard_map.80.refs_7_ = f32[256,4096]{1,0:T(8,128)} custom-call(bf16[256,512]{1,0:T(8,128)(2,1)S(1)} %pad_maximum_fusion.1.refs_0_, bf16[256,512]{1,0:T(8,128)(2,1)S(1)} %pad_maximum_fusion.2.refs_1_, f32[1,4096]{1,0:T(1,128)S(1)} %copy-done.3, bf16[256,4096]{1,0:T(8,128)(2,1)S(1)} %bitcast.19, bf16[256,4096]{1,0:T(8,128)(2,1)} %collective-permute-done.5.refs_4_, ...), custom_call_target="tpu_custom_call" | custom-call | flops 1073741824 | bytes 6815744 | tf_op jit(solution)/shard_map/pallas_call | solution.py:248
  130.5 0.0 collective-permute-done.8
  130.5 0.6 add.107
  131.1 0.0 collective-permute-done.7.refs_6_
  131.1 0.5 collective-permute-start.11
  131.6 2.3 %collective-permute-done.11.refs_5_ = bf16[256,2048]{1,0:T(8,128)(2,1)S(1)} collective-permute-done((bf16[256,2048]{1,0:T(8,128)(2,1)S(1)}, bf16[256,2048]{1,0:T(8,128)(2,1)S(1)}, u32[]{:S(2)}, u32[]{:S(2)}) %collective-permute-start.11) | collective-permute-done | bytes 1048608 | tf_op jit(solution)/shard_map/ppermute | solution.py:54
  133.9 4.4 %shard_map.81 = f32[256,4096]{1,0:T(8,128)} custom-call(bf16[256,512]{1,0:T(8,128)(2,1)S(1)} %pad_maximum_fusion.1.refs_0_, bf16[256,512]{1,0:T(8,128)(2,1)S(1)} %pad_maximum_fusion.2.refs_1_, f32[1,4096]{1,0:T(1,128)S(1)} %copy-done.3, bf16[256,4096]{1,0:T(8,128)(2,1)S(1)} %bitcast.20, ...), custom_call_target="tpu_custom_call", output_to_operand_aliasing={{}: (7, {})} | custom-call | flops 1073741824 | bytes 6815744 | tf_op jit(solution)/shard_map/pallas_call | solution.py:248
  (7 shorter events, 0.1 us)
Async XLA Ops:
  65.3 36.0 %collective-permute-start.9 = (bf16[256,2048]{1,0:T(8,128)(2,1)}, bf16[256,2048]{1,0:T(8,128)(2,1)}, u32[]{:S(2)}, u32[]{:S(2)}) collective-permute-start(bf16[256,2048]{1,0:T(8,128)(2,1)} %get-tuple-element.19), channel_id=1, source_target_pairs={{0,16},{8,24},{16,0},{24,8},{1,17},{9,25},{17,1},{25,9},{2,18},{10... | collective-permute-start | bytes 3145736 | tf_op jit(solution)/shard_map/ppermute | solution.py:54
  68.3 49.3 %collective-permute-start.1 = (bf16[256,4096]{1,0:T(8,128)(2,1)}, bf16[256,4096]{1,0:T(8,128)(2,1)}, u32[]{:S(2)}, u32[]{:S(2)}) collective-permute-start(bf16[256,4096]{1,0:T(8,128)(2,1)} %bitcast.27), channel_id=1, source_target_pairs={{2,0},{4,2},{6,4},{3,1},{5,3},{7,5},{10,8},{12,10},{14,12},{11,9},... | collective-permute-start | bytes 6291464 | tf_op jit(solution)/shard_map/ppermute | solution.py:281
  69.6 10.1 %copy-start = (bf16[1,256,4096]{2,1,0:T(8,128)(2,1)S(1)}, bf16[1,256,4096]{2,1,0:T(8,128)(2,1)}, u32[]{:S(2)}) copy-start(bf16[1,256,4096]{2,1,0:T(8,128)(2,1)} %param.5) | copy-start | bytes 6291460
  79.7 46.0 %collective-permute-start.5 = (bf16[256,4096]{1,0:T(8,128)(2,1)S(1)}, bf16[256,4096]{1,0:T(8,128)(2,1)}, u32[]{:S(2)}, u32[]{:S(2)}) collective-permute-start(bf16[256,4096]{1,0:T(8,128)(2,1)S(1)} %bitcast.18), channel_id=1, source_target_pairs={{0,8},{8,0},{16,24},{24,16},{1,9},{9,1},{17,25},{25,17},{2,10},{10... | collective-permute-start | bytes 6291464 | tf_op jit(solution)/shard_map/ppermute | solution.py:54
  79.7 3.7 %collective-permute-start = (f32[2,256]{1,0:T(2,128)}, f32[2,256]{1,0:T(2,128)S(1)}, u32[]{:S(2)}, u32[]{:S(2)}) collective-permute-start(f32[2,256]{1,0:T(2,128)} %get-tuple-element.16.refs_0_), channel_id=1, source_target_pairs={{0,1},{1,0},{2,3},{3,2},{4,5},{5,4},{6,7},{7,6},{8,9},{9,8},{10,11... | collective-permute-start | bytes 6152 | tf_op jit(solution)/shard_map/ppermute | solution.py:37
  83.5 0.6 copy-start.4
  93.7 1.6 %collective-permute-start.2 = (bf16[2,256,256]{2,1,0:T(8,128)(2,1)S(1)}, bf16[2,256,256]{2,1,0:T(8,128)(2,1)S(1)}, u32[]{:S(2)}, u32[]{:S(2)}) collective-permute-start(bf16[2,256,256]{2,1,0:T(8,128)(2,1)S(1)} %pad_maximum_fusion), channel_id=1, source_target_pairs={{0,8},{8,0},{16,24},{24,16},{1,9},{9,1},{17,25},{25,17},{2,10},{10... | collective-permute-start | bytes 786440 | tf_op jit(solution)/shard_map/ppermute | solution.py:54
  95.4 5.9 %collective-permute-start.3 = (bf16[256,256]{1,0:T(8,128)(2,1)S(1)}, bf16[256,256]{1,0:T(8,128)(2,1)S(1)}, u32[]{:S(2)}, u32[]{:S(2)}) collective-permute-start(bf16[256,256]{1,0:T(8,128)(2,1)S(1)} %fusion), channel_id=1, source_target_pairs={{0,24},{8,16},{16,8},{24,0},{1,25},{9,17},{17,9},{25,1},{2,26},{10... | collective-permute-start | bytes 393224 | tf_op jit(solution)/shard_map/ppermute | solution.py:54
  95.5 5.8 %collective-permute-start.6 = (f32[1,4096]{1,0:T(1,128)}, f32[1,4096]{1,0:T(1,128)S(1)}, u32[]{:S(2)}, u32[]{:S(2)}) collective-permute-start(f32[1,4096]{1,0:T(1,128)} %get-tuple-element.24), channel_id=1, source_target_pairs={{0,24},{8,16},{16,8},{24,0},{1,25},{9,17},{17,9},{25,1},{2,26},{10... | collective-permute-start | bytes 49160 | tf_op jit(solution)/shard_map/ppermute | solution.py:54
  101.3 24.4 %collective-permute-start.10 = (bf16[256,2048]{1,0:T(8,128)(2,1)}, bf16[256,2048]{1,0:T(8,128)(2,1)}, u32[]{:S(2)}, u32[]{:S(2)}) collective-permute-start(bf16[256,2048]{1,0:T(8,128)(2,1)} %collective-permute-done.9.refs_6_), channel_id=1, source_target_pairs={{0,8},{8,0},{16,24},{24,16},{1,9},{9,1},{17,25},{25,17},{2,10},{10... | collective-permute-start | bytes 3145736 | tf_op jit(solution)/shard_map/ppermute | solution.py:54
  101.8 29.3 %collective-permute-start.7 = (bf16[256,2048]{1,0:T(8,128)(2,1)}, bf16[256,2048]{1,0:T(8,128)(2,1)S(1)}, u32[]{:S(2)}, u32[]{:S(2)}) collective-permute-start(bf16[256,2048]{1,0:T(8,128)(2,1)} %get-tuple-element.25), channel_id=1, source_target_pairs={{0,16},{8,24},{16,0},{24,8},{1,17},{9,25},{17,1},{25,9},{2,18},{10... | collective-permute-start | bytes 3145736 | tf_op jit(solution)/shard_map/ppermute | solution.py:54
  102.6 5.6 %collective-permute-start.4 = (bf16[256,256]{1,0:T(8,128)(2,1)S(1)}, bf16[256,256]{1,0:T(8,128)(2,1)S(1)}, u32[]{:S(2)}, u32[]{:S(2)}) collective-permute-start(bf16[256,256]{1,0:T(8,128)(2,1)S(1)} %collective-permute-done.3), channel_id=1, source_target_pairs={{0,1},{1,0},{2,3},{3,2},{4,5},{5,4},{6,7},{7,6},{8,9},{9,8},{10,11... | collective-permute-start | bytes 393224 | tf_op jit(solution)/shard_map/ppermute | solution.py:37
  117.6 2.2 %copy-start.2 = (f32[256,4096]{1,0:T(8,128)S(1)}, f32[256,4096]{1,0:T(8,128)}, u32[]{:S(2)}) copy-start(f32[256,4096]{1,0:T(8,128)} %get-tuple-element.18.local_ref) | copy-start | bytes 12582916
  119.8 5.9 %copy-start.1 = (bf16[1,256,4096]{2,1,0:T(8,128)(2,1)S(1)}, bf16[1,256,4096]{2,1,0:T(8,128)(2,1)}, u32[]{:S(2)}) copy-start(bf16[1,256,4096]{2,1,0:T(8,128)(2,1)} %param.5) | copy-start | bytes 6291460
  119.8 5.9 %copy-start.3 = (f32[1,4096]{1,0:T(1,128)S(1)}, f32[1,4096]{1,0:T(1,128)}, u32[]{:S(2)}) copy-start(f32[1,4096]{1,0:T(1,128)} %refs_2_.3) | copy-start | bytes 49156
  125.7 4.8 %collective-permute-start.8 = (f32[1,4096]{1,0:T(1,128)S(1)}, f32[1,4096]{1,0:T(1,128)S(1)}, u32[]{:S(2)}, u32[]{:S(2)}) collective-permute-start(f32[1,4096]{1,0:T(1,128)S(1)} %add.106), channel_id=1, source_target_pairs={{0,8},{8,0},{16,24},{24,16},{1,9},{9,1},{17,25},{25,17},{2,10},{10... | collective-permute-start | bytes 49160 | tf_op jit(solution)/shard_map/ppermute | solution.py:54
  131.1 2.8 %collective-permute-start.11 = (bf16[256,2048]{1,0:T(8,128)(2,1)S(1)}, bf16[256,2048]{1,0:T(8,128)(2,1)S(1)}, u32[]{:S(2)}, u32[]{:S(2)}) collective-permute-start(bf16[256,2048]{1,0:T(8,128)(2,1)S(1)} %collective-permute-done.7.refs_6_), channel_id=1, source_target_pairs={{0,8},{8,0},{16,24},{24,16},{1,9},{9,1},{17,25},{25,17},{2,10},{10... | collective-permute-start | bytes 3145736 | tf_op jit(solution)/shard_map/ppermute | solution.py:54
